TPU v7x, 32 devices: a whole 2x2x4 slice. The times are simulated.
32 devices in a mesh: rep: 2 (over x), row: 4 (over y, core), col: 4 (over z).
Axes of the slice: x: 2, y: 2, z: 4, core: 2. Of those that a mesh axis runs over, the one named last changes fastest.
Arguments:
- tokens: bfloat16 [4096, 2048], P(('rep', 'row', 'col')), may hold values from -18 to 18
- norm_gain: float32 [2048], replicated, may hold values from 0.1 to 1.9
- gate_weights: float32 [4096, 6], P(('rep', 'row', 'col')), may hold values from 0.05 to 0.5
- routes: int32 [4096, 6], P(('rep', 'row', 'col')), may hold values from 0 to 63, all different within a row; in each aligned block of 128 rows (0 to 127, 128 to 255, ...) at most 18 rows name the same one
- moves: int32 [16, 2, 32], P(('row', 'col')), may hold values from 0 to 127, as said below
- w_gate: bfloat16 [64, 2048, 1408], P(('row', 'col')), may hold values from -0.125 to 0.125
- w_up: bfloat16 [64, 2048, 1408], P(('row', 'col')), may hold values from -0.125 to 0.125
- w_down: bfloat16 [64, 1408, 2048], P(('row', 'col')), may hold values from -0.15625 to 0.15625
Outputs:
- served: bfloat16 [4096, 2048], P(('rep', 'row', 'col'))
Inputs may be any that keep to these rules, and one draw needn't show every extreme that they name: `routes`: in the 128 rows of one device no expert is named by more than 18 rows, a bound that some block reaches. For each p, moves[p, 0] holds 32 different rows and moves[p, 1] holds 32 different rows.
All inputs are finite; a program needn't handle non-finite values.
Results may differ from a plain program's by a relative error of at most 0.0037.
Values may be sent and summed in bfloat16 or wider, within the bound.
No kernel may reach another device: no remote copies, remote signals or barrier semaphores. Data moves between devices by JAX's collectives and lax.ppermute only.
A program may use at most 128 MiB of HBM per device.

v0:
```python
import functools

import jax
import jax.numpy as jnp
from jax import lax
from jax.experimental import pallas as pl
from jax.experimental.pallas import tpu as pltpu
from jax.sharding import PartitionSpec as P

GROUP = 8
PIECES = 4
LANE = 8
WIDE = 512
NARROW = 512
LIMIT = 60 * 1024 * 1024
LIGHT = pl.CostEstimate(flops=1, bytes_accessed=1, transcendentals=0)


def shifted(value, axis, steps):
    count = lax.axis_size(axis)
    first, last = (max(0, -steps), min(count, count - steps))
    return lax.ppermute(value, axis, [(source, source + steps) for source in range(first, last)])


def turned(value, steps):
    count = lax.axis_size("col")
    return lax.ppermute(value, "col", [(source, (source + steps) % count) for source in range(count)])


def swapped(value, bit):
    count = lax.axis_size("row")
    return lax.ppermute(value, "row", [(source, source ^ bit) for source in range(count)])


def spread(halves, gather):
    line, other, last = [halves], [], halves
    for _ in range(1, lax.axis_size("col")):
        pairs = [lax.optimization_barrier((turned(one, 1), swapped(one, 2))) for one in last]
        last = [ahead for ahead, _ in pairs]
        line.append(last)
        other.append([across for _, across in pairs])
    ready = gather(line + [[swapped(one, 1) for one in block] for block in line])
    final = [swapped(one, 2) for one in last]
    held = lax.optimization_barrier((*final, ready[2]))[: len(final)]
    far = [[swapped(one, 1) for one in block] for block in other + [list(held)]]
    return ready, other + [final] + far


def added(*parts):
    return sum(part.astype(jnp.float32) for part in parts).astype(jnp.bfloat16)


def collected(late, early):
    cols = lax.axis_size("col")
    order = list(range(cols // 2, 0, -1)) + list(range(cols // 2 + 1, cols)) + [0]
    held = {step: swapped(late[cols + step], 1) for step in order}
    sent = {step: swapped(added(late[step], held[step]), 2) for step in order}
    far = {
        step: swapped(lax.optimization_barrier((early[cols + step], held[step]))[0], 1)
        for step in order
    }
    line = [[early[step], far[step], sent[step]] for step in range(cols)]
    down, up = [], []
    for step in range(cols // 2, 0, -1):
        down = [turned(added(*(line[step] + down)), -1)]
        if step == cols // 2:
            ahead = down[0]
    for step in range(cols // 2 + 1, cols):
        value = added(*(line[step] + up))
        if not up:
            value = lax.optimization_barrier((value, ahead))[0]
        up = [turned(value, 1)]
    return line[0] + up + down


def head_kernel(tokens_ref, gain_ref, weights_ref, routes_ref, *outs):
    features, per_token = tokens_ref.shape[1], routes_ref.shape[0]
    widened = tokens_ref[...].astype(jnp.float32)
    scale = lax.rsqrt(jnp.mean(widened * widened, axis=-1, keepdims=True) + 1e-06)
    normed = (widened * scale * gain_ref[...]).astype(jnp.bfloat16)
    half = outs[0].shape[0]
    for i, out_ref in enumerate(outs):
        out_ref[:, :features] = normed[i * half : (i + 1) * half]
    weights = weights_ref[...]
    high = weights.astype(jnp.bfloat16).astype(jnp.float32)
    middle = (weights - high).astype(jnp.bfloat16).astype(jnp.float32)
    low = weights - high - middle
    gap = jnp.zeros((LANE - per_token, weights.shape[1]), jnp.float32)
    meta = [routes_ref[...].astype(jnp.float32), gap - 1.0, high, gap, middle, gap, low, gap]
    outs[0][: 4 * LANE, features:] = jnp.concatenate(meta, axis=0).astype(jnp.bfloat16)
    outs[0][4 * LANE :, features:] = jnp.zeros(
        (half - 4 * LANE, weights.shape[1]), jnp.bfloat16
    )


def gather_groups(xs, first, slots, xbuf, xsem, named_s, weight_s, pbuf, tbuf, put_weight, put_rows, begin=None):
    groups = len(xs) // (2 * GROUP)
    half = xs[0].shape[0]
    tok = 2 * half
    features = xs[1].shape[1]
    pairs = named_s.shape[0]
    exp_dev = pairs // GROUP

    def copies(g):
        for b in range(GROUP):
            for h in range(2):
                source = xs[2 * (g * GROUP + b) + h]
                target = xbuf.at[
                    g % 2, pl.ds(b * tok + h * half, half), pl.ds(0, source.shape[1])
                ]
                yield pltpu.make_async_copy(source, target, xsem.at[g % 2, 2 * b + h])

    def load(g):
        for copy in copies(g):
            copy.start()

    for g in range(min(2, groups)):
        load(g)
    if begin is not None:
        begin()
    lane = lax.broadcasted_iota(jnp.int32, (tok, tok), 1)
    sub = lax.broadcasted_iota(jnp.int32, (tok, tok), 0)
    upto = (sub <= lane).astype(jnp.bfloat16)
    pair_r = lax.broadcasted_iota(jnp.int32, (pairs, pairs), 0)
    pair_c = lax.broadcasted_iota(jnp.int32, (pairs, pairs), 1)
    before = ((pair_r // GROUP == pair_c // GROUP) & (pair_c < pair_r)).astype(jnp.bfloat16)
    slot_id = lax.broadcasted_iota(jnp.int32, (slots, tok), 0).astype(jnp.float32)
    wide_id = lax.broadcasted_iota(jnp.int32, (tok, exp_dev * slots), 1).astype(jnp.float32)
    offset = lax.broadcasted_iota(jnp.int32, (pairs, tok), 0) // GROUP * slots
    offset = offset.astype(jnp.float32)

    for g in range(groups):
        for copy in copies(g):
            copy.wait()
        for b in range(GROUP):
            meta = xbuf[g % 2, b * tok : b * tok + 4 * LANE, features:].astype(jnp.float32)
            chosen = meta[:LANE]
            given = meta[LANE : 2 * LANE] + meta[2 * LANE : 3 * LANE] + meta[3 * LANE : 4 * LANE]
            for e in range(exp_dev):
                hit = chosen == (first + e).astype(jnp.float32)
                named_s[e * GROUP + b : e * GROUP + b + 1, :] = jnp.sum(
                    hit.astype(jnp.float32), axis=0, keepdims=True
                )
                weight_s[e * GROUP + b : e * GROUP + b + 1, :] = jnp.sum(
                    jnp.where(hit, given, 0.0), axis=0, keepdims=True
                )
        named = named_s[...]
        count = jnp.dot(named.astype(jnp.bfloat16), upto, preferred_element_type=jnp.float32)
        totals = jnp.broadcast_to(count[:, tok - 1 :], (pairs, tok)).astype(jnp.bfloat16)
        base = jnp.dot(before, totals, preferred_element_type=jnp.float32)
        named_s[...] = jnp.where(named > 0.5, base + count - 1.0, -1.0)
        for e in range(exp_dev):
            total = jnp.zeros((slots, tok), jnp.float32)
            for b in range(GROUP):
                pick = slot_id == named_s[e * GROUP + b : e * GROUP + b + 1, :]
                pbuf[e * slots : (e + 1) * slots, b * tok : (b + 1) * tok] = pick.astype(
                    jnp.float32
                ).astype(jnp.bfloat16)
                total += jnp.where(pick, weight_s[e * GROUP + b : e * GROUP + b + 1, :], 0.0)
            put_weight(g, e, jnp.sum(total, axis=1, keepdims=True))
        place = named_s[...]
        place = jnp.where(place < -0.5, place, place + offset)
        place = jnp.concatenate([place, jnp.zeros((tok - pairs, tok), jnp.float32)], axis=0).T
        for b in range(GROUP):
            pick = wide_id == place[:, b : b + 1]
            for e in range(1, exp_dev):
                pick = pick | (wide_id == place[:, e * GROUP + b : e * GROUP + b + 1])
            tbuf[g, b * tok : (b + 1) * tok, :] = pick.astype(jnp.float32).astype(jnp.bfloat16)

        @pl.loop(0, features // WIDE)
        def _(n):
            cols = pl.ds(pl.multiple_of(n * WIDE, WIDE), WIDE)
            got = jnp.dot(pbuf[...], xbuf[g % 2, :, cols], preferred_element_type=jnp.float32)
            got = got.astype(jnp.bfloat16)
            for e in range(exp_dev):
                put_rows(g, e, cols, got[e * slots : (e + 1) * slots])

        if g + 2 < groups:
            load(g + 2)


def early_kernel(plan, first_ref, *refs):
    nb, slots = plan
    xs, refs = refs[: 2 * nb], refs[2 * nb :]
    rows_ref, tbuf, slotw, xbuf, pbuf, named_s, weight_s, xsem = refs

    def put_weight(g, e, value):
        slotw[e, g * slots : (g + 1) * slots, :] = value

    def put_rows(g, e, cols, value):
        rows_ref[e, g * slots : (g + 1) * slots, cols] = value

    gather_groups(
        xs, first_ref[0], slots, xbuf, xsem, named_s, weight_s, pbuf, tbuf, put_weight, put_rows
    )


def expert_kernel(plan, first_ref, *refs):
    nb, exp_dev, slots, tiles = plan
    xs, refs = refs[: 2 * nb], refs[2 * nb :]
    rows_ref, table_ref, slotw_ref, gate_ref, up_ref, down_ref = refs[:6]
    outs, refs = refs[6 : 6 + 2 * nb], refs[6 + 2 * nb :]
    gate_b, up_b, down_b, xbuf, gbuf, pbuf, tbuf, act, obuf, stage, slotw = refs[:11]
    named_s, weight_s, wsem, downsem, xsem, osem, rsem, tsem = refs[11:]
    groups = nb // GROUP
    tok, features = outs[0].shape
    early = groups * slots
    steps = features // WIDE

    def pieces_start(source, target, sem):
        size = target.shape[0] // PIECES
        for piece in range(PIECES):
            part = pl.ds(piece * size, size)
            copy = pltpu.make_async_copy(source.at[part, :], target.at[part, :], sem)
            copy.start(priority=piece % 2)

    def weight_refs(kind, e, slot):
        source, target = ((gate_ref, gate_b), (up_ref, up_b))[kind]
        return source.at[e], target.at[slot], wsem.at[kind, slot]

    def down_refs(n, e):
        source = down_ref.at[e, :, pl.ds(n * WIDE, WIDE)]
        return source, down_b.at[n % 2, e], downsem.at[n % 2, e]

    def fetch(e, slot):
        for kind in range(2):
            pieces_start(*weight_refs(kind, e, slot))

    def fetch_down(n):
        for e in range(exp_dev):
            pieces_start(*down_refs(n, e))

    def arrive(kind, e, slot):
        pltpu.make_async_copy(*weight_refs(kind, e, slot)).wait()

    def rows_copy(e):
        return pltpu.make_async_copy(rows_ref.at[e], gbuf.at[e, pl.ds(0, early), :], rsem.at[e])

    def out_copy(n, g, b):
        return pltpu.make_async_copy(
            stage.at[n % 2, g, pl.ds(b * tok, tok), :],
            outs[g * GROUP + b].at[:, pl.ds(n * WIDE, WIDE)],
            osem.at[n % 2, g, b],
        )

    table_in = pltpu.make_async_copy(table_ref, tbuf.at[pl.ds(groups, groups)], tsem)

    def put_weight(g, e, value):
        slotw[e, early + g * slots : early + (g + 1) * slots, :] = value

    def put_rows(g, e, cols, value):
        gbuf[e, early + g * slots : early + (g + 1) * slots, cols] = value

    def begin():
        pieces_start(*weight_refs(0, 0, 0))
        for e in range(exp_dev):
            rows_copy(e).start()
        pieces_start(*weight_refs(1, 0, 0))
        if exp_dev > 1:
            fetch(1, 1)
        table_in.start()
        for n in range(min(2, steps)):
            fetch_down(n)
        slotw[:, :early, :] = slotw_ref[...]

    gather_groups(
        xs,
        first_ref[0],
        slots,
        xbuf,
        xsem,
        named_s,
        weight_s,
        pbuf,
        tbuf,
        put_weight,
        put_rows,
        begin,
    )

    @pl.loop(0, exp_dev)
    def _(e):
        slot = lax.rem(e, gate_b.shape[0])
        rows_copy(e).wait()
        arrive(0, e, slot)
        arrive(1, e, slot)
        for start, size in tiles:
            gate = jnp.dot(
                gbuf[e], gate_b[slot, :, start : start + size], preferred_element_type=jnp.float32
            )
            upward = jnp.dot(
                gbuf[e], up_b[slot, :, start : start + size], preferred_element_type=jnp.float32
            )
            act[e, :, start : start + size] = (
                0.5 * gate * (1.0 + jnp.tanh(0.5 * gate)) * upward * slotw[e]
            ).astype(jnp.bfloat16)

        @pl.when(e + 2 < exp_dev)
        def _():
            fetch(e + 2, slot)

    table_in.wait()
    for n in range(steps):
        for e in range(exp_dev):
            pltpu.make_async_copy(*down_refs(n, e)).wait()
            obuf[e] = jnp.dot(
                act[e], down_b[n % 2, e], preferred_element_type=jnp.float32
            ).astype(jnp.bfloat16)
        if n + 2 < steps:
            fetch_down(n + 2)
        for g in range(2 * groups):
            if n >= 2:
                for b in range(GROUP):
                    out_copy(n - 2, g, b).wait()
            here = (groups + g if g < groups else g - groups) * slots
            made = jnp.concatenate(
                [obuf[e, here : here + slots, :] for e in range(exp_dev)], axis=0
            )
            stage[n % 2, g] = jnp.dot(
                tbuf[g], made, preferred_element_type=jnp.float32
            ).astype(jnp.bfloat16)
            for b in range(GROUP):
                out_copy(n, g, b).start()
    for n in range(max(0, steps - 2), steps):
        for g in range(2 * groups):
            for b in range(GROUP):
                out_copy(n, g, b).wait()


def sizes(blocks, capacity, exp_dev):
    slots = -(-GROUP * capacity // 16) * 16
    return len(blocks), 2 * blocks[0][0].shape[0], slots, len(blocks) // GROUP, exp_dev * GROUP


def scratch(tok, features, exp_dev, slots, groups):
    return [
        pltpu.VMEM((min(2, groups), GROUP * tok, features + tok), jnp.bfloat16),
        pltpu.VMEM((exp_dev * slots, GROUP * tok), jnp.bfloat16),
        pltpu.VMEM((exp_dev * GROUP, tok), jnp.float32),
    ]


def gathered(blocks, first, capacity, exp_dev):
    nb, tok, slots, groups, _ = sizes(blocks, capacity, exp_dev)
    features = blocks[0][1].shape[1]
    xbuf, pbuf, small = scratch(tok, features, exp_dev, slots, groups)
    return pl.pallas_call(
        functools.partial(early_kernel, (nb, slots)),
        out_shape=[
            jax.ShapeDtypeStruct((exp_dev, groups * slots, features), jnp.bfloat16),
            jax.ShapeDtypeStruct((groups, GROUP * tok, exp_dev * slots), jnp.bfloat16),
            jax.ShapeDtypeStruct((exp_dev, groups * slots, 1), jnp.float32),
        ],
        in_specs=[pl.BlockSpec(memory_space=pltpu.SMEM)]
        + [pl.BlockSpec(memory_space=pl.ANY)] * (2 * nb),
        grid=(1,),
        out_specs=[
            pl.BlockSpec((exp_dev, groups * slots, features), lambda i: (0, 0, 0)),
            pl.BlockSpec((groups, GROUP * tok, exp_dev * slots), lambda i: (0, 0, 0)),
            pl.BlockSpec((exp_dev, groups * slots, 1), lambda i: (0, 0, 0)),
        ],
        scratch_shapes=[xbuf, pbuf, small, small, pltpu.SemaphoreType.DMA((2, 2 * GROUP))],
        compiler_params=pltpu.CompilerParams(vmem_limit_bytes=LIMIT),
        cost_estimate=LIGHT,
        name="early",
    )(first, *[half for block in blocks for half in block])


def experts_of(ready, late, first, capacity, w_gate, w_up, w_down):
    rows, table, slotw = ready
    exp_dev, features, hidden = w_gate.shape
    nb, tok, slots, groups, pairs = sizes(late, capacity, exp_dev)
    every = 2 * groups * slots
    held = min(2, exp_dev)
    tiles = [(start, min(NARROW, hidden - start)) for start in range(0, hidden, NARROW)]
    smem = pl.BlockSpec(memory_space=pltpu.SMEM)
    anywhere = pl.BlockSpec(memory_space=pl.ANY)
    xbuf, pbuf, small = scratch(tok, features, exp_dev, slots, groups)
    tbuf = pltpu.VMEM((2 * groups,) + table.shape[1:], jnp.bfloat16)
    act = pltpu.VMEM((exp_dev, every, hidden), jnp.bfloat16)
    blocks = [jax.ShapeDtypeStruct((tok, features), jnp.bfloat16)] * (2 * nb)
    got = pl.pallas_call(
        functools.partial(expert_kernel, (nb, exp_dev, slots, tiles)),
        grid=(1,),
        out_shape=blocks,
        in_specs=[smem]
        + [anywhere] * (2 * nb + 2)
        + [pl.BlockSpec(slotw.shape, lambda i: (0, 0, 0))]
        + [anywhere] * 3,
        out_specs=[anywhere] * (2 * nb),
        scratch_shapes=[
            pltpu.VMEM((held, features, hidden), jnp.bfloat16),
            pltpu.VMEM((held, features, hidden), jnp.bfloat16),
            pltpu.VMEM((2, exp_dev, hidden, WIDE), jnp.bfloat16),
            xbuf,
            pltpu.VMEM((exp_dev, every, features), jnp.bfloat16),
            pbuf,
            tbuf,
            act,
            pltpu.VMEM((exp_dev, every, WIDE), jnp.bfloat16),
            pltpu.VMEM((2, 2 * groups, GROUP * tok, WIDE), jnp.bfloat16),
            pltpu.VMEM((exp_dev, every, 1), jnp.float32),
            small,
            small,
            pltpu.SemaphoreType.DMA((2, held)),
            pltpu.SemaphoreType.DMA((2, exp_dev)),
            pltpu.SemaphoreType.DMA((2, 2 * GROUP)),
            pltpu.SemaphoreType.DMA((2, 2 * groups, GROUP)),
            pltpu.SemaphoreType.DMA((exp_dev,)),
            pltpu.SemaphoreType.DMA,
        ],
        compiler_params=pltpu.CompilerParams(vmem_limit_bytes=LIMIT),
        cost_estimate=pl.CostEstimate(
            flops=6 * exp_dev * every * features * hidden,
            bytes_accessed=6 * exp_dev * features * hidden + 4 * nb * tok * features,
            transcendentals=0,
        ),
        name="experts",
    )(first, *[half for block in late for half in block], rows, table, slotw, w_gate, w_up, w_down)
    return list(got[:nb]), list(got[nb:])


def body(tokens, norm_gain, gate_weights, routes, moves, w_gate, w_up, w_down):
    tok_rows, features = tokens.shape
    per_token = routes.shape[1]
    exp_dev = w_gate.shape[0]
    group = lax.axis_size("row") * lax.axis_size("col")
    experts = group * exp_dev
    capacity = tok_rows * per_token * 3 // (2 * experts)
    half = tok_rows // 2
    halves = pl.pallas_call(
        head_kernel,
        out_shape=[
            jax.ShapeDtypeStruct((half, features + tok_rows), jnp.bfloat16),
            jax.ShapeDtypeStruct((half, features), jnp.bfloat16),
        ],
        name="head",
    )(tokens, norm_gain.reshape(1, features), gate_weights.T, routes.T)
    first = (lax.axis_index(("row", "col")) * exp_dev).astype(jnp.int32).reshape(1)
    ready, late = spread(
        list(halves), lambda blocks: gathered(blocks, first, capacity, exp_dev)
    )
    late, early = experts_of(ready, late, first, capacity, w_gate, w_up, w_down)
    total = added(tokens, *collected(late, early))
    rows = jnp.arange(tok_rows, dtype=jnp.int32)
    pick = (moves[0, 0][:, None] == rows[None, :]).astype(jnp.bfloat16)
    leaving = jnp.dot(pick, total, preferred_element_type=jnp.float32).astype(jnp.bfloat16)
    incoming = shifted(leaving, "rep", 1)
    second = lax.axis_index("rep") == 1
    target = jnp.where(second, moves[0, 1], moves[0, 0])
    match = rows[:, None] == target[None, :]
    placed = jnp.dot(match.astype(jnp.bfloat16), incoming, preferred_element_type=jnp.float32)
    placed = jnp.where(second, placed, 0.0).astype(jnp.bfloat16)
    return jnp.where(jnp.any(match, axis=1, keepdims=True), placed, total)


def solution(mesh):
    return jax.shard_map(
        body,
        mesh=mesh,
        in_specs=(
            P(("rep", "row", "col"), None),
            P(),
            P(("rep", "row", "col"), None),
            P(("rep", "row", "col"), None),
            P(("row", "col"), None, None),
            P(("row", "col"), None, None),
            P(("row", "col"), None, None),
            P(("row", "col"), None, None),
        ),
        out_specs=P(("rep", "row", "col"), None),
        check_vma=False,
    )
```

profile of v0, /device:TPU:0, one launch (start us, length us, event | category | flops | bytes accessed | tf_op | source)
XLA Modules:
  0.0 179.5 jit_solution(3224676661956899358)
XLA Ops:
  0.0 2.0 %head.1 = (bf16[64,2176]{1,0:T(8,128)(2,1)}, bf16[64,2048]{1,0:T(8,128)(2,1)}) custom-call(bf16[128,2048]{1,0:T(8,128)(2,1)} %tokens_ref.1, f32[1,2048]{1,0:T(1,128)} %bitcast.12, f32[6,128]{1,0:T(8,128)} %bitcast.13, s32[6,128]{1,0:T(8,128)} %bitcast.14), custom_call_target="tpu_custom_call" | custom-call | tf_op jit(solution)/shard_map/head/pallas_call | solution.py:431
  2.0 3.0 %collective-permute-start.2 = (bf16[64,2048]{1,0:T(8,128)(2,1)}, bf16[64,2048]{1,0:T(8,128)(2,1)S(1)}, u32[]{:S(2)}, u32[]{:S(2)}) collective-permute-start(bf16[64,2048]{1,0:T(8,128)(2,1)} %get-tuple-element.47.refs_1_), channel_id=1, source_target_pairs={{0,1},{1,2},{2,3},{3,0},{4,5},{5,6},{6,7},{7,4},{8,9},{9,10},{10,1... | collective-permute-start | bytes 786440 | tf_op jit(solution)/shard_map/ppermute | solution.py:27
  5.1 1.5 collective-permute-start.3
  6.6 1.6 collective-permute-start
  8.2 0.5 collective-permute-start.1
  8.7 5.8 %collective-permute-done.2.refs_3_ = bf16[64,2048]{1,0:T(8,128)(2,1)S(1)} collective-permute-done((bf16[64,2048]{1,0:T(8,128)(2,1)}, bf16[64,2048]{1,0:T(8,128)(2,1)S(1)}, u32[]{:S(2)}, u32[]{:S(2)}) %collective-permute-start.2) | collective-permute-done | bytes 262176 | tf_op jit(solution)/shard_map/ppermute | solution.py:27
  14.6 1.6 collective-permute-start.6
  16.2 1.5 collective-permute-start.7
  17.7 2.7 %collective-permute-done.refs_2_ = bf16[64,2176]{1,0:T(8,128)(2,1)S(1)} collective-permute-done((bf16[64,2176]{1,0:T(8,128)(2,1)}, bf16[64,2176]{1,0:T(8,128)(2,1)S(1)}, u32[]{:S(2)}, u32[]{:S(2)}) %collective-permute-start) | collective-permute-done | bytes 278560 | tf_op jit(solution)/shard_map/ppermute | solution.py:27
  20.5 1.6 collective-permute-start.4
  22.1 1.5 collective-permute-start.5
  23.6 2.4 %collective-permute-done.6.refs_5_ = bf16[64,2048]{1,0:T(8,128)(2,1)S(1)} collective-permute-done((bf16[64,2048]{1,0:T(8,128)(2,1)S(1)}, bf16[64,2048]{1,0:T(8,128)(2,1)S(1)}, u32[]{:S(2)}, u32[]{:S(2)}) %collective-permute-start.6) | collective-permute-done | bytes 262176 | tf_op jit(solution)/shard_map/ppermute | solution.py:27
  26.2 1.6 collective-permute-start.10
  27.8 1.5 collective-permute-start.11
  29.3 2.7 %collective-permute-done.4.refs_4_ = bf16[64,2176]{1,0:T(8,128)(2,1)S(1)} collective-permute-done((bf16[64,2176]{1,0:T(8,128)(2,1)S(1)}, bf16[64,2176]{1,0:T(8,128)(2,1)S(1)}, u32[]{:S(2)}, u32[]{:S(2)}) %collective-permute-start.4) | collective-permute-done | bytes 278560 | tf_op jit(solution)/shard_map/ppermute | solution.py:27
  32.1 1.6 collective-permute-start.8
  33.6 1.5 collective-permute-start.9
  35.2 2.5 %collective-permute-done.10.refs_7_ = bf16[64,2048]{1,0:T(8,128)(2,1)} collective-permute-done((bf16[64,2048]{1,0:T(8,128)(2,1)S(1)}, bf16[64,2048]{1,0:T(8,128)(2,1)}, u32[]{:S(2)}, u32[]{:S(2)}) %collective-permute-start.10) | collective-permute-done | bytes 262176 | tf_op jit(solution)/shard_map/ppermute | solution.py:27
  37.8 0.4 collective-permute-start.22
  38.2 4.5 %collective-permute-done.8.refs_6_ = bf16[64,2176]{1,0:T(8,128)(2,1)S(1)} collective-permute-done((bf16[64,2176]{1,0:T(8,128)(2,1)S(1)}, bf16[64,2176]{1,0:T(8,128)(2,1)S(1)}, u32[]{:S(2)}, u32[]{:S(2)}) %collective-permute-start.8) | collective-permute-done | bytes 278560 | tf_op jit(solution)/shard_map/ppermute | solution.py:27
  42.8 0.5 collective-permute-start.25
  43.4 0.4 collective-permute-start.27
  43.8 1.5 collective-permute-start.12
  45.3 0.9 collective-permute-start.13
  46.2 0.5 collective-permute-start.15
  47.0 0.4 copy-done.7
  47.4 8.9 %early.1 = (bf16[4,144,2048]{2,1,0:T(8,128)(2,1)}, bf16[1,1024,576]{2,1,0:T(8,128)(2,1)}, f32[4,144,1]{2,1,0:T(8,128)}) custom-call(s32[1]{0:T(128)} %bitcast.2.first_ref, bf16[64,2176]{1,0:T(8,128)(2,1)} %get-tuple-element.45.refs_0_, bf16[64,2048]{1,0:T(8,128)(2,1)} %get-tuple-element.47.refs_1_, bf16[64,2176]{1,0:T(8,128)(2,1)} %copy-done.1, ...), custom_call_target="tpu_custom_call" | custom-call | flops 1 | bytes 1 | tf_op jit(solution)/shard_map/early/pallas_call | solution.py:347
  56.4 1.8 %collective-permute-done.13.refs_7_ = bf16[64,2048]{1,0:T(8,128)(2,1)} collective-permute-done((bf16[64,2048]{1,0:T(8,128)(2,1)}, bf16[64,2048]{1,0:T(8,128)(2,1)}, u32[]{:S(2)}, u32[]{:S(2)}) %collective-permute-start.13) | collective-permute-done | bytes 262176 | tf_op jit(solution)/shard_map/ppermute | solution.py:32
  58.2 0.5 collective-permute-start.18
  58.8 0.4 collective-permute-start.19
  59.3 0.4 collective-permute-done.16.refs_10_
  59.7 1.4 collective-permute-done.19.refs_13_
  61.1 0.4 collective-permute-done.29.refs_15_
  61.5 0.2 copy-done.16
  61.9 0.3 copy-done.17
  62.3 48.3 %experts.1 = (bf16[128,2048]{1,0:T(8,128)(2,1)}, bf16[128,2048]{1,0:T(8,128)(2,1)}, bf16[128,2048]{1,0:T(8,128)(2,1)}, bf16[128,2048]{1,0:T(8,128)(2,1)}, bf16[1...) custom-call(s32[1]{0:T(128)} %bitcast.2.first_ref, ...), custom_call_target="tpu_custom_call" | custom-call | flops 19931332608 | bytes 77594624 | tf_op jit(solution)/shard_map/experts/pallas_call | solution.py:382
  110.8 0.4 collective-permute-start.36
  111.4 0.4 collective-permute-start.41
  111.7 1.1 collective-permute-done.33
  113.0 0.6 collective-permute-done.36
  113.7 1.2 add_convert_fusion.4
  114.9 1.6 collective-permute-start.38
  116.5 1.2 add_convert_fusion.6
  117.7 0.6 collective-permute-start.35
  118.2 1.2 add_convert_fusion.2
  119.5 10.2 %collective-permute-done.38 = bf16[128,2048]{1,0:T(8,128)(2,1)S(1)} collective-permute-done((bf16[128,2048]{1,0:T(8,128)(2,1)S(1)}, bf16[128,2048]{1,0:T(8,128)(2,1)S(1)}, u32[]{:S(2)}, u32[]{:S(2)}) %collective-permute-start.38) | collective-permute-done | bytes 524320 | tf_op jit(solution)/shard_map/ppermute | solution.py:32
  129.7 1.5 collective-permute-start.43
  131.2 1.3 add_convert_fusion.3
  132.5 1.8 %collective-permute-start.39 = (bf16[128,2048]{1,0:T(8,128)(2,1)S(1)}, bf16[128,2048]{1,0:T(8,128)(2,1)S(1)}, u32[]{:S(2)}, u32[]{:S(2)}) collective-permute-start(bf16[128,2048]{1,0:T(8,128)(2,1)S(1)} %add_convert_fusion.3), channel_id=1, source_target_pairs={{0,3},{1,0},{2,1},{3,2},{4,7},{5,4},{6,5},{7,6},{8,11},{9,8},{10,9... | collective-permute-start | bytes 1572872 | tf_op jit(solution)/shard_map/ppermute | solution.py:27
  134.3 1.2 add_convert_fusion.7
  135.6 5.4 %collective-permute-done.35 = bf16[128,2048]{1,0:T(8,128)(2,1)S(1)} collective-permute-done((bf16[128,2048]{1,0:T(8,128)(2,1)S(1)}, bf16[128,2048]{1,0:T(8,128)(2,1)S(1)}, u32[]{:S(2)}, u32[]{:S(2)}) %collective-permute-start.35) | collective-permute-done | bytes 524320 | tf_op jit(solution)/shard_map/ppermute | solution.py:32
  140.9 1.5 collective-permute-start.32
  142.5 2.1 %add_convert_fusion.5 = bf16[128,2048]{1,0:T(8,128)(2,1)} fusion(bf16[128,2048]{1,0:T(8,128)(2,1)S(1)} %collective-permute-done.35, bf16[128,2048]{1,0:T(8,128)(2,1)S(1)} %collective-permute-done.34, bf16[128,2048]{1,0:T(8,128)(2,1)} %get-tuple-element.69), kind=kLoop, calls=%fused_computation.9 | loop fusion | flops 1572864 | bytes 2097152 | tf_op jit(solution)/shard_map/convert_element_type | solution.py:50
  144.5 0.6 collective-permute-done.39
  145.1 0.9 collective-permute-start.40
  146.1 6.1 %collective-permute-done.43 = bf16[128,2048]{1,0:T(8,128)(2,1)S(1)} collective-permute-done((bf16[128,2048]{1,0:T(8,128)(2,1)S(1)}, bf16[128,2048]{1,0:T(8,128)(2,1)S(1)}, u32[]{:S(2)}, u32[]{:S(2)}) %collective-permute-start.43) | collective-permute-done | bytes 524320 | tf_op jit(solution)/shard_map/ppermute | solution.py:32
  152.2 2.2 %add_convert_fusion.1 = bf16[128,2048]{1,0:T(8,128)(2,1)} fusion(bf16[128,2048]{1,0:T(8,128)(2,1)S(1)} %collective-permute-done.39, bf16[128,2048]{1,0:T(8,128)(2,1)S(1)} %collective-permute-done.43, bf16[128,2048]{1,0:T(8,128)(2,1)S(1)} %collective-permute-done.42, bf16[128,2048]{1,0:T(8,128)(2,1)} %get-tuple-element.80), kind=kLoop, calls=%fused_computation.5 | loop fusion | flops 2097152 | bytes 2621440 | tf_op jit(solution)/shard_map/convert_element_type | solution.py:50
  154.3 1.7 collective-permute-start.44
  156.1 6.8 %collective-permute-done.32 = bf16[128,2048]{1,0:T(8,128)(2,1)S(1)} collective-permute-done((bf16[128,2048]{1,0:T(8,128)(2,1)S(1)}, bf16[128,2048]{1,0:T(8,128)(2,1)S(1)}, u32[]{:S(2)}, u32[]{:S(2)}) %collective-permute-start.32) | collective-permute-done | bytes 524320 | tf_op jit(solution)/shard_map/ppermute | solution.py:32
  162.9 7.5 %collective-permute-done.44 = bf16[128,2048]{1,0:T(8,128)(2,1)S(1)} collective-permute-done((bf16[128,2048]{1,0:T(8,128)(2,1)}, bf16[128,2048]{1,0:T(8,128)(2,1)S(1)}, u32[]{:S(2)}, u32[]{:S(2)}) %collective-permute-start.44) | collective-permute-done | bytes 524320 | tf_op jit(solution)/shard_map/ppermute | solution.py:27
  170.3 1.5 add_convert_fusion
  172.1 3.4 %collective-permute-start.45 = (bf16[32,2048]{1,0:T(8,128)(2,1)S(1)}, bf16[32,2048]{1,0:T(8,128)(2,1)S(1)}, u32[]{:S(2)}, u32[]{:S(2)}) collective-permute-start(bf16[32,2048]{1,0:T(8,128)(2,1)S(1)} %convolution_convert_fusion), channel_id=1, source_target_pairs={{0,16},{1,17},{2,18},{3,19},{4,20},{5,21},{6,22},{7,23},{8,24},{9,... | collective-permute-start | bytes 393224 | tf_op jit(solution)/shard_map/ppermute | solution.py:22
  175.7 2.6 %collective-permute-done.45 = bf16[32,2048]{1,0:T(8,128)(2,1)S(1)} collective-permute-done((bf16[32,2048]{1,0:T(8,128)(2,1)S(1)}, bf16[32,2048]{1,0:T(8,128)(2,1)S(1)}, u32[]{:S(2)}, u32[]{:S(2)}) %collective-permute-start.45) | collective-permute-done | bytes 131104 | tf_op jit(solution)/shard_map/ppermute | solution.py:22
  178.3 1.2 fusion.1
  (92 shorter events, 2.5 us)
Async XLA Ops:
  2.0 12.4 %collective-permute-start.2 = (bf16[64,2048]{1,0:T(8,128)(2,1)}, bf16[64,2048]{1,0:T(8,128)(2,1)S(1)}, u32[]{:S(2)}, u32[]{:S(2)}) collective-permute-start(bf16[64,2048]{1,0:T(8,128)(2,1)} %get-tuple-element.47.refs_1_), channel_id=1, source_target_pairs={{0,1},{1,2},{2,3},{3,0},{4,5},{5,6},{6,7},{7,4},{8,9},{9,10},{10,1... | collective-permute-start | bytes 786440 | tf_op jit(solution)/shard_map/ppermute | solution.py:27
  5.1 9.5 %collective-permute-start.3 = (bf16[64,2048]{1,0:T(8,128)(2,1)}, bf16[64,2048]{1,0:T(8,128)(2,1)}, u32[]{:S(2)}, u32[]{:S(2)}) collective-permute-start(bf16[64,2048]{1,0:T(8,128)(2,1)} %get-tuple-element.47.refs_1_), channel_id=1, source_target_pairs={{0,8},{4,12},{8,0},{12,4},{1,9},{5,13},{9,1},{13,5},{2,10},{6,14},... | collective-permute-start | bytes 786440 | tf_op jit(solution)/shard_map/ppermute | solution.py:32
  6.6 13.8 %collective-permute-start = (bf16[64,2176]{1,0:T(8,128)(2,1)}, bf16[64,2176]{1,0:T(8,128)(2,1)S(1)}, u32[]{:S(2)}, u32[]{:S(2)}) collective-permute-start(bf16[64,2176]{1,0:T(8,128)(2,1)} %get-tuple-element.45.refs_0_), channel_id=1, source_target_pairs={{0,1},{1,2},{2,3},{3,0},{4,5},{5,6},{6,7},{7,4},{8,9},{9,10},{10,1... | collective-permute-start | bytes 835592 | tf_op jit(solution)/shard_map/ppermute | solution.py:27
  8.2 12.3 %collective-permute-start.1 = (bf16[64,2176]{1,0:T(8,128)(2,1)}, bf16[64,2176]{1,0:T(8,128)(2,1)S(1)}, u32[]{:S(2)}, u32[]{:S(2)}) collective-permute-start(bf16[64,2176]{1,0:T(8,128)(2,1)} %get-tuple-element.45.refs_0_), channel_id=1, source_target_pairs={{0,8},{4,12},{8,0},{12,4},{1,9},{5,13},{9,1},{13,5},{2,10},{6,14},... | collective-permute-start | bytes 835592 | tf_op jit(solution)/shard_map/ppermute | solution.py:32
  14.4 32.3 %copy-start.18 = (bf16[64,2048]{1,0:T(8,128)(2,1)}, bf16[64,2048]{1,0:T(8,128)(2,1)S(1)}, u32[]{:S(2)}) copy-start(bf16[64,2048]{1,0:T(8,128)(2,1)S(1)} %collective-permute-done.2.refs_3_) | copy-start | bytes 786436
  14.6 11.4 %collective-permute-start.6 = (bf16[64,2048]{1,0:T(8,128)(2,1)S(1)}, bf16[64,2048]{1,0:T(8,128)(2,1)S(1)}, u32[]{:S(2)}, u32[]{:S(2)}) collective-permute-start(bf16[64,2048]{1,0:T(8,128)(2,1)S(1)} %collective-permute-done.2.refs_3_), channel_id=1, source_target_pairs={{0,1},{1,2},{2,3},{3,0},{4,5},{5,6},{6,7},{7,4},{8,9},{9,10},{10,1... | collective-permute-start | bytes 786440 | tf_op jit(solution)/shard_map/ppermute | solution.py:27
  16.2 10.0 %collective-permute-start.7 = (bf16[64,2048]{1,0:T(8,128)(2,1)S(1)}, bf16[64,2048]{1,0:T(8,128)(2,1)}, u32[]{:S(2)}, u32[]{:S(2)}) collective-permute-start(bf16[64,2048]{1,0:T(8,128)(2,1)S(1)} %collective-permute-done.2.refs_3_), channel_id=1, source_target_pairs={{0,8},{4,12},{8,0},{12,4},{1,9},{5,13},{9,1},{13,5},{2,10},{6,14},... | collective-permute-start | bytes 786440 | tf_op jit(solution)/shard_map/ppermute | solution.py:32
  20.4 26.6 %copy-start.1 = (bf16[64,2176]{1,0:T(8,128)(2,1)}, bf16[64,2176]{1,0:T(8,128)(2,1)S(1)}, u32[]{:S(2)}) copy-start(bf16[64,2176]{1,0:T(8,128)(2,1)S(1)} %collective-permute-done.refs_2_) | copy-start | bytes 835588
  20.5 41.0 %copy-start.8 = (bf16[64,2176]{1,0:T(8,128)(2,1)}, bf16[64,2176]{1,0:T(8,128)(2,1)S(1)}, u32[]{:S(2)}) copy-start(bf16[64,2176]{1,0:T(8,128)(2,1)S(1)} %collective-permute-done.1.refs_0_) | copy-start | bytes 835588
  20.5 11.5 %collective-permute-start.4 = (bf16[64,2176]{1,0:T(8,128)(2,1)S(1)}, bf16[64,2176]{1,0:T(8,128)(2,1)S(1)}, u32[]{:S(2)}, u32[]{:S(2)}) collective-permute-start(bf16[64,2176]{1,0:T(8,128)(2,1)S(1)} %collective-permute-done.refs_2_), channel_id=1, source_target_pairs={{0,1},{1,2},{2,3},{3,0},{4,5},{5,6},{6,7},{7,4},{8,9},{9,10},{10,1... | collective-permute-start | bytes 835592 | tf_op jit(solution)/shard_map/ppermute | solution.py:27
  22.1 10.0 %collective-permute-start.5 = (bf16[64,2176]{1,0:T(8,128)(2,1)S(1)}, bf16[64,2176]{1,0:T(8,128)(2,1)S(1)}, u32[]{:S(2)}, u32[]{:S(2)}) collective-permute-start(bf16[64,2176]{1,0:T(8,128)(2,1)S(1)} %collective-permute-done.refs_2_), channel_id=1, source_target_pairs={{0,8},{4,12},{8,0},{12,4},{1,9},{5,13},{9,1},{13,5},{2,10},{6,14},... | collective-permute-start | bytes 835592 | tf_op jit(solution)/shard_map/ppermute | solution.py:32
  23.6 11.6 %collective-permute-start.21 = (bf16[64,2048]{1,0:T(8,128)(2,1)}, bf16[64,2048]{1,0:T(8,128)(2,1)}, u32[]{:S(2)}, u32[]{:S(2)}) collective-permute-start(bf16[64,2048]{1,0:T(8,128)(2,1)} %get-tuple-element.47.refs_1_), channel_id=1, source_target_pairs={{0,4},{4,0},{8,12},{12,8},{1,5},{5,1},{9,13},{13,9},{2,6},{6,2},{1... | collective-permute-start | bytes 786440 | tf_op jit(solution)/shard_map/ppermute | solution.py:32
  26.0 20.9 %copy-start.19 = (bf16[64,2048]{1,0:T(8,128)(2,1)}, bf16[64,2048]{1,0:T(8,128)(2,1)S(1)}, u32[]{:S(2)}) copy-start(bf16[64,2048]{1,0:T(8,128)(2,1)S(1)} %collective-permute-done.6.refs_5_) | copy-start | bytes 786436
  26.2 11.5 %collective-permute-start.10 = (bf16[64,2048]{1,0:T(8,128)(2,1)S(1)}, bf16[64,2048]{1,0:T(8,128)(2,1)}, u32[]{:S(2)}, u32[]{:S(2)}) collective-permute-start(bf16[64,2048]{1,0:T(8,128)(2,1)S(1)} %collective-permute-done.6.refs_5_), channel_id=1, source_target_pairs={{0,1},{1,2},{2,3},{3,0},{4,5},{5,6},{6,7},{7,4},{8,9},{9,10},{10,1... | collective-permute-start | bytes 786440 | tf_op jit(solution)/shard_map/ppermute | solution.py:27
  27.8 10.0 %collective-permute-start.11 = (bf16[64,2048]{1,0:T(8,128)(2,1)S(1)}, bf16[64,2048]{1,0:T(8,128)(2,1)}, u32[]{:S(2)}, u32[]{:S(2)}) collective-permute-start(bf16[64,2048]{1,0:T(8,128)(2,1)S(1)} %collective-permute-done.6.refs_5_), channel_id=1, source_target_pairs={{0,8},{4,12},{8,0},{12,4},{1,9},{5,13},{9,1},{13,5},{2,10},{6,14},... | collective-permute-start | bytes 786440 | tf_op jit(solution)/shard_map/ppermute | solution.py:32
  32.0 15.0 %copy-start.2 = (bf16[64,2176]{1,0:T(8,128)(2,1)}, bf16[64,2176]{1,0:T(8,128)(2,1)S(1)}, u32[]{:S(2)}) copy-start(bf16[64,2176]{1,0:T(8,128)(2,1)S(1)} %collective-permute-done.4.refs_4_) | copy-start | bytes 835588
  32.1 29.4 %copy-start.9 = (bf16[64,2176]{1,0:T(8,128)(2,1)}, bf16[64,2176]{1,0:T(8,128)(2,1)S(1)}, u32[]{:S(2)}) copy-start(bf16[64,2176]{1,0:T(8,128)(2,1)S(1)} %collective-permute-done.5.refs_2_) | copy-start | bytes 835588
  32.1 10.7 %collective-permute-start.8 = (bf16[64,2176]{1,0:T(8,128)(2,1)S(1)}, bf16[64,2176]{1,0:T(8,128)(2,1)S(1)}, u32[]{:S(2)}, u32[]{:S(2)}) collective-permute-start(bf16[64,2176]{1,0:T(8,128)(2,1)S(1)} %collective-permute-done.4.refs_4_), channel_id=1, source_target_pairs={{0,1},{1,2},{2,3},{3,0},{4,5},{5,6},{6,7},{7,4},{8,9},{9,10},{10,1... | collective-permute-start | bytes 835592 | tf_op jit(solution)/shard_map/ppermute | solution.py:27
  33.6 9.1 %collective-permute-start.9 = (bf16[64,2176]{1,0:T(8,128)(2,1)S(1)}, bf16[64,2176]{1,0:T(8,128)(2,1)S(1)}, u32[]{:S(2)}, u32[]{:S(2)}) collective-permute-start(bf16[64,2176]{1,0:T(8,128)(2,1)S(1)} %collective-permute-done.4.refs_4_), channel_id=1, source_target_pairs={{0,8},{4,12},{8,0},{12,4},{1,9},{5,13},{9,1},{13,5},{2,10},{6,14},... | collective-permute-start | bytes 835592 | tf_op jit(solution)/shard_map/ppermute | solution.py:32
  35.2 8.1 %collective-permute-start.20 = (bf16[64,2176]{1,0:T(8,128)(2,1)}, bf16[64,2176]{1,0:T(8,128)(2,1)S(1)}, u32[]{:S(2)}, u32[]{:S(2)}) collective-permute-start(bf16[64,2176]{1,0:T(8,128)(2,1)} %get-tuple-element.45.refs_0_), channel_id=1, source_target_pairs={{0,4},{4,0},{8,12},{12,8},{1,5},{5,1},{9,13},{13,9},{2,6},{6,2},{1... | collective-permute-start | bytes 835592 | tf_op jit(solution)/shard_map/ppermute | solution.py:32
  37.7 5.6 %collective-permute-start.23 = (bf16[64,2048]{1,0:T(8,128)(2,1)S(1)}, bf16[64,2048]{1,0:T(8,128)(2,1)S(1)}, u32[]{:S(2)}, u32[]{:S(2)}) collective-permute-start(bf16[64,2048]{1,0:T(8,128)(2,1)S(1)} %collective-permute-done.2.refs_3_), channel_id=1, source_target_pairs={{0,4},{4,0},{8,12},{12,8},{1,5},{5,1},{9,13},{13,9},{2,6},{6,2},{1... | collective-permute-start | bytes 786440 | tf_op jit(solution)/shard_map/ppermute | solution.py:32
  37.8 6.0 %collective-permute-start.22 = (bf16[64,2176]{1,0:T(8,128)(2,1)S(1)}, bf16[64,2176]{1,0:T(8,128)(2,1)S(1)}, u32[]{:S(2)}, u32[]{:S(2)}) collective-permute-start(bf16[64,2176]{1,0:T(8,128)(2,1)S(1)} %collective-permute-done.refs_2_), channel_id=1, source_target_pairs={{0,4},{4,0},{8,12},{12,8},{1,5},{5,1},{9,13},{13,9},{2,6},{6,2},{1... | collective-permute-start | bytes 835592 | tf_op jit(solution)/shard_map/ppermute | solution.py:32
  42.7 4.2 %copy-start.3 = (bf16[64,2176]{1,0:T(8,128)(2,1)}, bf16[64,2176]{1,0:T(8,128)(2,1)S(1)}, u32[]{:S(2)}) copy-start(bf16[64,2176]{1,0:T(8,128)(2,1)S(1)} %collective-permute-done.8.refs_6_) | copy-start | bytes 835588
  42.7 3.5 %collective-permute-start.24 = (bf16[64,2176]{1,0:T(8,128)(2,1)S(1)}, bf16[64,2176]{1,0:T(8,128)(2,1)S(1)}, u32[]{:S(2)}, u32[]{:S(2)}) collective-permute-start(bf16[64,2176]{1,0:T(8,128)(2,1)S(1)} %collective-permute-done.4.refs_4_), channel_id=1, source_target_pairs={{0,4},{4,0},{8,12},{12,8},{1,5},{5,1},{9,13},{13,9},{2,6},{6,2},{1... | collective-permute-start | bytes 835592 | tf_op jit(solution)/shard_map/ppermute | solution.py:32
  42.8 18.7 %copy-start.10 = (bf16[64,2176]{1,0:T(8,128)(2,1)}, bf16[64,2176]{1,0:T(8,128)(2,1)S(1)}, u32[]{:S(2)}) copy-start(bf16[64,2176]{1,0:T(8,128)(2,1)S(1)} %collective-permute-done.9.refs_4_) | copy-start | bytes 835588
  42.8 2.5 %collective-permute-start.25 = (bf16[64,2048]{1,0:T(8,128)(2,1)S(1)}, bf16[64,2048]{1,0:T(8,128)(2,1)S(1)}, u32[]{:S(2)}, u32[]{:S(2)}) collective-permute-start(bf16[64,2048]{1,0:T(8,128)(2,1)S(1)} %collective-permute-done.6.refs_5_), channel_id=1, source_target_pairs={{0,4},{4,0},{8,12},{12,8},{1,5},{5,1},{9,13},{13,9},{2,6},{6,2},{1... | collective-permute-start | bytes 786440 | tf_op jit(solution)/shard_map/ppermute | solution.py:32
  43.3 3.7 %copy-start.4 = (bf16[64,2176]{1,0:T(8,128)(2,1)}, bf16[64,2176]{1,0:T(8,128)(2,1)S(1)}, u32[]{:S(2)}) copy-start(bf16[64,2176]{1,0:T(8,128)(2,1)S(1)} %collective-permute-done.20.refs_8_) | copy-start | bytes 835588
  43.3 3.5 %collective-permute-start.26 = (bf16[64,2176]{1,0:T(8,128)(2,1)S(1)}, bf16[64,2176]{1,0:T(8,128)(2,1)S(1)}, u32[]{:S(2)}, u32[]{:S(2)}) collective-permute-start(bf16[64,2176]{1,0:T(8,128)(2,1)S(1)} %collective-permute-done.8.refs_6_), channel_id=1, source_target_pairs={{0,4},{4,0},{8,12},{12,8},{1,5},{5,1},{9,13},{13,9},{2,6},{6,2},{1... | collective-permute-start | bytes 835592 | tf_op jit(solution)/shard_map/ppermute | solution.py:32
  43.4 3.5 %copy-start.20 = (bf16[64,2048]{1,0:T(8,128)(2,1)}, bf16[64,2048]{1,0:T(8,128)(2,1)S(1)}, u32[]{:S(2)}) copy-start(bf16[64,2048]{1,0:T(8,128)(2,1)S(1)} %collective-permute-done.23.refs_11_) | copy-start | bytes 786436
  43.4 2.9 %collective-permute-start.27 = (bf16[64,2048]{1,0:T(8,128)(2,1)}, bf16[64,2048]{1,0:T(8,128)(2,1)S(1)}, u32[]{:S(2)}, u32[]{:S(2)}) collective-permute-start(bf16[64,2048]{1,0:T(8,128)(2,1)} %collective-permute-done.10.refs_7_), channel_id=1, source_target_pairs={{0,4},{4,0},{8,12},{12,8},{1,5},{5,1},{9,13},{13,9},{2,6},{6,2},{1... | collective-permute-start | bytes 786440 | tf_op jit(solution)/shard_map/ppermute | solution.py:32
  43.8 3.2 %copy-start.5 = (bf16[64,2176]{1,0:T(8,128)(2,1)}, bf16[64,2176]{1,0:T(8,128)(2,1)S(1)}, u32[]{:S(2)}) copy-start(bf16[64,2176]{1,0:T(8,128)(2,1)S(1)} %collective-permute-done.22.refs_10_) | copy-start | bytes 835588
  43.8 14.4 %collective-permute-start.12 = (bf16[64,2176]{1,0:T(8,128)(2,1)S(1)}, bf16[64,2176]{1,0:T(8,128)(2,1)S(1)}, u32[]{:S(2)}, u32[]{:S(2)}) collective-permute-start(bf16[64,2176]{1,0:T(8,128)(2,1)S(1)} %collective-permute-done.8.refs_6_), channel_id=1, source_target_pairs={{0,8},{4,12},{8,0},{12,4},{1,9},{5,13},{9,1},{13,5},{2,10},{6,14},... | collective-permute-start | bytes 835592 | tf_op jit(solution)/shard_map/ppermute | solution.py:32
  45.3 1.6 copy-start.21
  45.3 12.8 %collective-permute-start.13 = (bf16[64,2048]{1,0:T(8,128)(2,1)}, bf16[64,2048]{1,0:T(8,128)(2,1)}, u32[]{:S(2)}, u32[]{:S(2)}) collective-permute-start(bf16[64,2048]{1,0:T(8,128)(2,1)} %collective-permute-done.10.refs_7_), channel_id=1, source_target_pairs={{0,8},{4,12},{8,0},{12,4},{1,9},{5,13},{9,1},{13,5},{2,10},{6,14},... | collective-permute-start | bytes 786440 | tf_op jit(solution)/shard_map/ppermute | solution.py:32
  46.2 12.6 %collective-permute-start.14 = (bf16[64,2176]{1,0:T(8,128)(2,1)S(1)}, bf16[64,2176]{1,0:T(8,128)(2,1)S(1)}, u32[]{:S(2)}, u32[]{:S(2)}) collective-permute-start(bf16[64,2176]{1,0:T(8,128)(2,1)S(1)} %collective-permute-done.1.refs_0_), channel_id=1, source_target_pairs={{0,4},{4,0},{8,12},{12,8},{1,5},{5,1},{9,13},{13,9},{2,6},{6,2},{1... | collective-permute-start | bytes 835592 | tf_op jit(solution)/shard_map/ppermute | solution.py:32
  46.2 12.4 %collective-permute-start.15 = (bf16[64,2048]{1,0:T(8,128)(2,1)}, bf16[64,2048]{1,0:T(8,128)(2,1)}, u32[]{:S(2)}, u32[]{:S(2)}) collective-permute-start(bf16[64,2048]{1,0:T(8,128)(2,1)} %collective-permute-done.3.refs_1_), channel_id=1, source_target_pairs={{0,4},{4,0},{8,12},{12,8},{1,5},{5,1},{9,13},{13,9},{2,6},{6,2},{1... | collective-permute-start | bytes 786440 | tf_op jit(solution)/shard_map/ppermute | solution.py:32
  46.7 12.5 %collective-permute-start.17 = (bf16[64,2048]{1,0:T(8,128)(2,1)}, bf16[64,2048]{1,0:T(8,128)(2,1)}, u32[]{:S(2)}, u32[]{:S(2)}) collective-permute-start(bf16[64,2048]{1,0:T(8,128)(2,1)} %collective-permute-done.7.refs_3_), channel_id=1, source_target_pairs={{0,4},{4,0},{8,12},{12,8},{1,5},{5,1},{9,13},{13,9},{2,6},{6,2},{1... | collective-permute-start | bytes 786440 | tf_op jit(solution)/shard_map/ppermute | solution.py:32
  58.2 1.6 collective-permute-start.16
  58.2 3.3 %copy-start.11 = (bf16[64,2176]{1,0:T(8,128)(2,1)}, bf16[64,2176]{1,0:T(8,128)(2,1)S(1)}, u32[]{:S(2)}) copy-start(bf16[64,2176]{1,0:T(8,128)(2,1)S(1)} %collective-permute-done.12.refs_6_) | copy-start | bytes 835588
  58.2 2.9 %collective-permute-start.18 = (bf16[64,2176]{1,0:T(8,128)(2,1)S(1)}, bf16[64,2176]{1,0:T(8,128)(2,1)S(1)}, u32[]{:S(2)}, u32[]{:S(2)}) collective-permute-start(bf16[64,2176]{1,0:T(8,128)(2,1)S(1)} %collective-permute-done.9.refs_4_), channel_id=1, source_target_pairs={{0,4},{4,0},{8,12},{12,8},{1,5},{5,1},{9,13},{13,9},{2,6},{6,2},{1... | collective-permute-start | bytes 835592 | tf_op jit(solution)/shard_map/ppermute | solution.py:32
  58.7 2.8 %collective-permute-start.28 = (bf16[64,2176]{1,0:T(8,128)(2,1)S(1)}, bf16[64,2176]{1,0:T(8,128)(2,1)S(1)}, u32[]{:S(2)}, u32[]{:S(2)}) collective-permute-start(bf16[64,2176]{1,0:T(8,128)(2,1)S(1)} %collective-permute-done.12.refs_6_), channel_id=1, source_target_pairs={{0,4},{4,0},{8,12},{12,8},{1,5},{5,1},{9,13},{13,9},{2,6},{6,2},{1... | collective-permute-start | bytes 835592 | tf_op jit(solution)/shard_map/ppermute | solution.py:32
  58.8 2.8 %copy-start.12 = (bf16[64,2176]{1,0:T(8,128)(2,1)}, bf16[64,2176]{1,0:T(8,128)(2,1)S(1)}, u32[]{:S(2)}) copy-start(bf16[64,2176]{1,0:T(8,128)(2,1)S(1)} %collective-permute-done.14.refs_8_) | copy-start | bytes 835588
  58.8 2.3 %collective-permute-start.19 = (bf16[64,2048]{1,0:T(8,128)(2,1)}, bf16[64,2048]{1,0:T(8,128)(2,1)S(1)}, u32[]{:S(2)}, u32[]{:S(2)}) collective-permute-start(bf16[64,2048]{1,0:T(8,128)(2,1)} %collective-permute-done.11.refs_5_), channel_id=1, source_target_pairs={{0,4},{4,0},{8,12},{12,8},{1,5},{5,1},{9,13},{13,9},{2,6},{6,2},{1... | collective-permute-start | bytes 786440 | tf_op jit(solution)/shard_map/ppermute | solution.py:32
  59.2 2.3 %collective-permute-start.29 = (bf16[64,2048]{1,0:T(8,128)(2,1)}, bf16[64,2048]{1,0:T(8,128)(2,1)S(1)}, u32[]{:S(2)}, u32[]{:S(2)}) collective-permute-start(bf16[64,2048]{1,0:T(8,128)(2,1)} %collective-permute-done.13.refs_7_), channel_id=1, source_target_pairs={{0,4},{4,0},{8,12},{12,8},{1,5},{5,1},{9,13},{13,9},{2,6},{6,2},{1... | collective-permute-start | bytes 786440 | tf_op jit(solution)/shard_map/ppermute | solution.py:32
  59.7 1.8 %copy-start.13 = (bf16[64,2176]{1,0:T(8,128)(2,1)}, bf16[64,2176]{1,0:T(8,128)(2,1)S(1)}, u32[]{:S(2)}) copy-start(bf16[64,2176]{1,0:T(8,128)(2,1)S(1)} %collective-permute-done.16.refs_10_) | copy-start | bytes 835588
  61.5 0.8 copy-start.15
  62.3 93.8 %copy-start.23 = (s32[1,2,32]{2,1,0:T(2,128)S(1)}, s32[1,2,32]{2,1,0:T(2,128)}, u32[]{:S(2)}) copy-start(s32[1,2,32]{2,1,0:T(2,128)} %param.12) | copy-start | bytes 772
  62.3 108.0 %copy-start = (bf16[128,2048]{1,0:T(8,128)(2,1)S(1)}, bf16[128,2048]{1,0:T(8,128)(2,1)}, u32[]{:S(2)}) copy-start(bf16[128,2048]{1,0:T(8,128)(2,1)} %tokens_ref.1) | copy-start | bytes 1572868
  110.6 2.2 %collective-permute-start.33 = (bf16[128,2048]{1,0:T(8,128)(2,1)}, bf16[128,2048]{1,0:T(8,128)(2,1)S(1)}, u32[]{:S(2)}, u32[]{:S(2)}) collective-permute-start(bf16[128,2048]{1,0:T(8,128)(2,1)} %get-tuple-element.71), channel_id=1, source_target_pairs={{0,4},{4,0},{8,12},{12,8},{1,5},{5,1},{9,13},{13,9},{2,6},{6,2},{1... | collective-permute-start | bytes 1572872 | tf_op jit(solution)/shard_map/ppermute | solution.py:32
  110.8 2.7 %collective-permute-start.36 = (bf16[128,2048]{1,0:T(8,128)(2,1)}, bf16[128,2048]{1,0:T(8,128)(2,1)S(1)}, u32[]{:S(2)}, u32[]{:S(2)}) collective-permute-start(bf16[128,2048]{1,0:T(8,128)(2,1)} %get-tuple-element.76), channel_id=1, source_target_pairs={{0,4},{4,0},{8,12},{12,8},{1,5},{5,1},{9,13},{13,9},{2,6},{6,2},{1... | collective-permute-start | bytes 1572872 | tf_op jit(solution)/shard_map/ppermute | solution.py:32
  111.2 21.3 %collective-permute-start.30 = (bf16[128,2048]{1,0:T(8,128)(2,1)}, bf16[128,2048]{1,0:T(8,128)(2,1)S(1)}, u32[]{:S(2)}, u32[]{:S(2)}) collective-permute-start(bf16[128,2048]{1,0:T(8,128)(2,1)} %get-tuple-element.66), channel_id=1, source_target_pairs={{0,4},{4,0},{8,12},{12,8},{1,5},{5,1},{9,13},{13,9},{2,6},{6,2},{1... | collective-permute-start | bytes 1572872 | tf_op jit(solution)/shard_map/ppermute | solution.py:32
  111.4 6.3 %collective-permute-start.41 = (bf16[128,2048]{1,0:T(8,128)(2,1)}, bf16[128,2048]{1,0:T(8,128)(2,1)S(1)}, u32[]{:S(2)}, u32[]{:S(2)}) collective-permute-start(bf16[128,2048]{1,0:T(8,128)(2,1)} %get-tuple-element.82), channel_id=1, source_target_pairs={{0,4},{4,0},{8,12},{12,8},{1,5},{5,1},{9,13},{13,9},{2,6},{6,2},{1... | collective-permute-start | bytes 1572872 | tf_op jit(solution)/shard_map/ppermute | solution.py:32
  112.8 22.7 %collective-permute-start.34 = (bf16[128,2048]{1,0:T(8,128)(2,1)}, bf16[128,2048]{1,0:T(8,128)(2,1)S(1)}, u32[]{:S(2)}, u32[]{:S(2)}) collective-permute-start(bf16[128,2048]{1,0:T(8,128)(2,1)} %get-tuple-element.72), channel_id=1, source_target_pairs={{0,4},{4,0},{8,12},{12,8},{1,5},{5,1},{9,13},{13,9},{2,6},{6,2},{1... | collective-permute-start | bytes 1572872 | tf_op jit(solution)/shard_map/ppermute | solution.py:32
  113.6 5.8 %collective-permute-start.37 = (bf16[128,2048]{1,0:T(8,128)(2,1)}, bf16[128,2048]{1,0:T(8,128)(2,1)S(1)}, u32[]{:S(2)}, u32[]{:S(2)}) collective-permute-start(bf16[128,2048]{1,0:T(8,128)(2,1)} %get-tuple-element.77), channel_id=1, source_target_pairs={{0,4},{4,0},{8,12},{12,8},{1,5},{5,1},{9,13},{13,9},{2,6},{6,2},{1... | collective-permute-start | bytes 1572872 | tf_op jit(solution)/shard_map/ppermute | solution.py:32
  114.9 14.8 %collective-permute-start.38 = (bf16[128,2048]{1,0:T(8,128)(2,1)S(1)}, bf16[128,2048]{1,0:T(8,128)(2,1)S(1)}, u32[]{:S(2)}, u32[]{:S(2)}) collective-permute-start(bf16[128,2048]{1,0:T(8,128)(2,1)S(1)} %add_convert_fusion.4), channel_id=1, source_target_pairs={{0,8},{4,12},{8,0},{12,4},{1,9},{5,13},{9,1},{13,5},{2,10},{6,14},... | collective-permute-start | bytes 1572872 | tf_op jit(solution)/shard_map/ppermute | solution.py:32
  117.7 23.3 %collective-permute-start.35 = (bf16[128,2048]{1,0:T(8,128)(2,1)S(1)}, bf16[128,2048]{1,0:T(8,128)(2,1)S(1)}, u32[]{:S(2)}, u32[]{:S(2)}) collective-permute-start(bf16[128,2048]{1,0:T(8,128)(2,1)S(1)} %add_convert_fusion.6), channel_id=1, source_target_pairs={{0,8},{4,12},{8,0},{12,4},{1,9},{5,13},{9,1},{13,5},{2,10},{6,14},... | collective-permute-start | bytes 1572872 | tf_op jit(solution)/shard_map/ppermute | solution.py:32
  119.4 26.6 %collective-permute-start.42 = (bf16[128,2048]{1,0:T(8,128)(2,1)}, bf16[128,2048]{1,0:T(8,128)(2,1)S(1)}, u32[]{:S(2)}, u32[]{:S(2)}) collective-permute-start(bf16[128,2048]{1,0:T(8,128)(2,1)} %get-tuple-element.83), channel_id=1, source_target_pairs={{0,4},{4,0},{8,12},{12,8},{1,5},{5,1},{9,13},{13,9},{2,6},{6,2},{1... | collective-permute-start | bytes 1572872 | tf_op jit(solution)/shard_map/ppermute | solution.py:32
  129.7 22.5 %collective-permute-start.43 = (bf16[128,2048]{1,0:T(8,128)(2,1)S(1)}, bf16[128,2048]{1,0:T(8,128)(2,1)S(1)}, u32[]{:S(2)}, u32[]{:S(2)}) collective-permute-start(bf16[128,2048]{1,0:T(8,128)(2,1)S(1)} %add_convert_fusion.2), channel_id=1, source_target_pairs={{0,8},{4,12},{8,0},{12,4},{1,9},{5,13},{9,1},{13,5},{2,10},{6,14},... | collective-permute-start | bytes 1572872 | tf_op jit(solution)/shard_map/ppermute | solution.py:32
  132.5 12.6 %collective-permute-start.39 = (bf16[128,2048]{1,0:T(8,128)(2,1)S(1)}, bf16[128,2048]{1,0:T(8,128)(2,1)S(1)}, u32[]{:S(2)}, u32[]{:S(2)}) collective-permute-start(bf16[128,2048]{1,0:T(8,128)(2,1)S(1)} %add_convert_fusion.3), channel_id=1, source_target_pairs={{0,3},{1,0},{2,1},{3,2},{4,7},{5,4},{6,5},{7,6},{8,11},{9,8},{10,9... | collective-permute-start | bytes 1572872 | tf_op jit(solution)/shard_map/ppermute | solution.py:27
  135.5 20.6 %collective-permute-start.31 = (bf16[128,2048]{1,0:T(8,128)(2,1)}, bf16[128,2048]{1,0:T(8,128)(2,1)S(1)}, u32[]{:S(2)}, u32[]{:S(2)}) collective-permute-start(bf16[128,2048]{1,0:T(8,128)(2,1)} %get-tuple-element.67), channel_id=1, source_target_pairs={{0,4},{4,0},{8,12},{12,8},{1,5},{5,1},{9,13},{13,9},{2,6},{6,2},{1... | collective-permute-start | bytes 1572872 | tf_op jit(solution)/shard_map/ppermute | solution.py:32
  140.9 21.9 %collective-permute-start.32 = (bf16[128,2048]{1,0:T(8,128)(2,1)S(1)}, bf16[128,2048]{1,0:T(8,128)(2,1)S(1)}, u32[]{:S(2)}, u32[]{:S(2)}) collective-permute-start(bf16[128,2048]{1,0:T(8,128)(2,1)S(1)} %add_convert_fusion.7), channel_id=1, source_target_pairs={{0,8},{4,12},{8,0},{12,4},{1,9},{5,13},{9,1},{13,5},{2,10},{6,14},... | collective-permute-start | bytes 1572872 | tf_op jit(solution)/shard_map/ppermute | solution.py:32
  145.1 17.7 %collective-permute-start.40 = (bf16[128,2048]{1,0:T(8,128)(2,1)}, bf16[128,2048]{1,0:T(8,128)(2,1)S(1)}, u32[]{:S(2)}, u32[]{:S(2)}) collective-permute-start(bf16[128,2048]{1,0:T(8,128)(2,1)} %add_convert_fusion.5), channel_id=1, source_target_pairs={{0,1},{1,2},{2,3},{3,0},{4,5},{5,6},{6,7},{7,4},{8,9},{9,10},{10,1... | collective-permute-start | bytes 1572872 | tf_op jit(solution)/shard_map/ppermute | solution.py:27
  154.3 16.0 %collective-permute-start.44 = (bf16[128,2048]{1,0:T(8,128)(2,1)}, bf16[128,2048]{1,0:T(8,128)(2,1)S(1)}, u32[]{:S(2)}, u32[]{:S(2)}) collective-permute-start(bf16[128,2048]{1,0:T(8,128)(2,1)} %add_convert_fusion.1), channel_id=1, source_target_pairs={{0,3},{1,0},{2,1},{3,2},{4,7},{5,4},{6,5},{7,6},{8,11},{9,8},{10,9... | collective-permute-start | bytes 1572872 | tf_op jit(solution)/shard_map/ppermute | solution.py:27
  172.1 6.2 %collective-permute-start.45 = (bf16[32,2048]{1,0:T(8,128)(2,1)S(1)}, bf16[32,2048]{1,0:T(8,128)(2,1)S(1)}, u32[]{:S(2)}, u32[]{:S(2)}) collective-permute-start(bf16[32,2048]{1,0:T(8,128)(2,1)S(1)} %convolution_convert_fusion), channel_id=1, source_target_pairs={{0,16},{1,17},{2,18},{3,19},{4,20},{5,21},{6,22},{7,23},{8,24},{9,... | collective-permute-start | bytes 393224 | tf_op jit(solution)/shard_map/ppermute | solution.py:22
  (6 other events, 4.5 us)
where the time goes:
time: 180 us
  waiting for transfers between devices  66.1 us (37%)
  Pallas kernels  59.3 us (33%)
  starting transfers between devices  39.2 us (22%)
  other arithmetic  11.8 us (7%)
    pallas_call x1, Pallas kernels, experts_of(): pl.pallas_call(functools.partial(expert_kernel, (nb, exp_dev, slots, tile...  48.3 us
    ppermute x36, waiting for transfers between devices, swapped(): lax.ppermute(value, 'row', [(source, source ^ bit) for source in range(co...  34.8 us
    ppermute x9, waiting for transfers between devices, turned(): lax.ppermute(value, 'col', [(source, (source + steps) % count) for source...  28.7 us
    ppermute x36, starting transfers between devices, swapped(): lax.ppermute(value, 'row', [(source, source ^ bit) for source in range(co...  20.4 us
    ppermute x9, starting transfers between devices, turned(): lax.ppermute(value, 'col', [(source, (source + steps) % count) for source...  15.4 us
    convert_element_type x8, other arithmetic, added(): sum((part.astype(jnp.float32) for part in parts)).astype(jnp.bfloat16)  11.7 us
    pallas_call x1, Pallas kernels, gathered(): pl.pallas_call(functools.partial(early_kernel, (nb, slots)), out_shape=[j...  8.91 us
  transfers between devices with their start and end apart: 46, of which 24 were waited for; matrix products, arithmetic and copies ran while one was open for 6% of the time, Pallas kernels for 5%

commit v1 on v0

--- a/solution.py
+++ b/solution.py
@@ -70,7 +70,7 @@
         if not up:
             value = lax.optimization_barrier((value, ahead))[0]
         up = [turned(value, 1)]
-    return line[0] + up + down
+    return line[0] + up, down[0]
 
 
 def head_kernel(tokens_ref, gain_ref, weights_ref, routes_ref, *outs):
@@ -441,10 +441,19 @@
         list(halves), lambda blocks: gathered(blocks, first, capacity, exp_dev)
     )
     late, early = experts_of(ready, late, first, capacity, w_gate, w_up, w_down)
-    total = added(tokens, *collected(late, early))
+    pieces, last = collected(late, early)
     rows = jnp.arange(tok_rows, dtype=jnp.int32)
     pick = (moves[0, 0][:, None] == rows[None, :]).astype(jnp.bfloat16)
-    leaving = jnp.dot(pick, total, preferred_element_type=jnp.float32).astype(jnp.bfloat16)
+    known = sum(piece.astype(jnp.float32) for piece in [tokens] + pieces)
+    picked = jnp.dot(
+        pick.astype(jnp.float32),
+        known,
+        precision=lax.Precision.HIGHEST,
+        preferred_element_type=jnp.float32,
+    )
+    leaving = jnp.dot(pick, last, preferred_element_type=jnp.float32)
+    leaving = (picked + leaving).astype(jnp.bfloat16)
+    total = (known + last.astype(jnp.float32)).astype(jnp.bfloat16)
     incoming = shifted(leaving, "rep", 1)
     second = lax.axis_index("rep") == 1
     target = jnp.where(second, moves[0, 1], moves[0, 0])

time: 180 us -> 181 us (level)
  matrix products: 1.45 us -> 5.77 us
  waiting for transfers between devices: 66.1 us -> 62.6 us
  other arithmetic: 11.8 us -> 9.48 us
  starting transfers between devices: 39.2 us -> 41.1 us
    ppermute x36, waiting for transfers between devices: 34.8 us -> 24.7 us  [swapped(): lax.ppermute(value, 'row', [(source, source ^ bit) for source in range(co...]
    ppermute x9, waiting for transfers between devices: 28.7 us -> 35.5 us  [turned(): lax.ppermute(value, 'col', [(source, (source + steps) % count) for source...]
    dot_general x1 -> x2, matrix products: 0.24 us -> 3.1 us  [the longest x1 1.81 us: body(): jnp.dot(pick.astype(jnp.float32), known, precision=lax.Precision.HIGHEST,...]
    convert_element_type x8 -> x7, other arithmetic: 11.7 us -> 9.39 us  [added(): sum((part.astype(jnp.float32) for part in parts)).astype(jnp.bfloat16)]
    ppermute x9, starting transfers between devices: 15.4 us -> 17.2 us  [turned(): lax.ppermute(value, 'col', [(source, (source + steps) % count) for source...]
where the time goes in v1:
time: 181 us; the launch traced here: 180 us
  waiting for transfers between devices  62.6 us (35%)
  Pallas kernels  59.3 us (33%)
  starting transfers between devices  41.1 us (23%)
  other arithmetic  9.48 us (5%)
  matrix products  5.77 us (3%)
    pallas_call x1, Pallas kernels, experts_of(): pl.pallas_call(functools.partial(expert_kernel, (nb, exp_dev, slots, tile...  48.4 us
    ppermute x9, waiting for transfers between devices, turned(): lax.ppermute(value, 'col', [(source, (source + steps) % count) for source...  35.5 us
    ppermute x36, waiting for transfers between devices, swapped(): lax.ppermute(value, 'row', [(source, source ^ bit) for source in range(co...  24.7 us
    ppermute x36, starting transfers between devices, swapped(): lax.ppermute(value, 'row', [(source, source ^ bit) for source in range(co...  20.5 us
    ppermute x9, starting transfers between devices, turned(): lax.ppermute(value, 'col', [(source, (source + steps) % count) for source...  17.2 us
    convert_element_type x7, other arithmetic, added(): sum((part.astype(jnp.float32) for part in parts)).astype(jnp.bfloat16)  9.39 us
    pallas_call x1, Pallas kernels, gathered(): pl.pallas_call(functools.partial(early_kernel, (nb, slots)), out_shape=[j...  8.91 us
  transfers between devices with their start and end apart: 46, of which 24 were waited for; matrix products, arithmetic and copies ran while one was open for 6% of the time, Pallas kernels for 5%

profile of v1, /device:TPU:0, one launch (start us, length us, event | category | flops | bytes accessed | tf_op | source)
XLA Modules:
  0.0 179.9 jit_solution(7105934182977547650)
XLA Ops:
  0.0 2.0 %head.1 = (bf16[64,2176]{1,0:T(8,128)(2,1)}, bf16[64,2048]{1,0:T(8,128)(2,1)}) custom-call(bf16[128,2048]{1,0:T(8,128)(2,1)} %tokens_ref.1, f32[1,2048]{1,0:T(1,128)} %bitcast.12, f32[6,128]{1,0:T(8,128)} %bitcast.13, s32[6,128]{1,0:T(8,128)} %bitcast.14), custom_call_target="tpu_custom_call" | custom-call | tf_op jit(solution)/shard_map/head/pallas_call | solution.py:431
  2.0 3.0 %collective-permute-start.2 = (bf16[64,2048]{1,0:T(8,128)(2,1)}, bf16[64,2048]{1,0:T(8,128)(2,1)S(1)}, u32[]{:S(2)}, u32[]{:S(2)}) collective-permute-start(bf16[64,2048]{1,0:T(8,128)(2,1)} %get-tuple-element.47.refs_1_), channel_id=1, source_target_pairs={{0,1},{1,2},{2,3},{3,0},{4,5},{5,6},{6,7},{7,4},{8,9},{9,10},{10,1... | collective-permute-start | bytes 786440 | tf_op jit(solution)/shard_map/ppermute | solution.py:27
  5.1 1.5 collective-permute-start.3
  6.6 1.6 collective-permute-start
  8.2 0.5 collective-permute-start.1
  8.7 5.8 %collective-permute-done.2.refs_3_ = bf16[64,2048]{1,0:T(8,128)(2,1)S(1)} collective-permute-done((bf16[64,2048]{1,0:T(8,128)(2,1)}, bf16[64,2048]{1,0:T(8,128)(2,1)S(1)}, u32[]{:S(2)}, u32[]{:S(2)}) %collective-permute-start.2) | collective-permute-done | bytes 262176 | tf_op jit(solution)/shard_map/ppermute | solution.py:27
  14.6 1.6 collective-permute-start.6
  16.2 1.5 collective-permute-start.7
  17.7 2.7 %collective-permute-done.refs_2_ = bf16[64,2176]{1,0:T(8,128)(2,1)S(1)} collective-permute-done((bf16[64,2176]{1,0:T(8,128)(2,1)}, bf16[64,2176]{1,0:T(8,128)(2,1)S(1)}, u32[]{:S(2)}, u32[]{:S(2)}) %collective-permute-start) | collective-permute-done | bytes 278560 | tf_op jit(solution)/shard_map/ppermute | solution.py:27
  20.5 1.6 collective-permute-start.4
  22.1 1.5 collective-permute-start.5
  23.6 2.4 %collective-permute-done.6.refs_5_ = bf16[64,2048]{1,0:T(8,128)(2,1)S(1)} collective-permute-done((bf16[64,2048]{1,0:T(8,128)(2,1)S(1)}, bf16[64,2048]{1,0:T(8,128)(2,1)S(1)}, u32[]{:S(2)}, u32[]{:S(2)}) %collective-permute-start.6) | collective-permute-done | bytes 262176 | tf_op jit(solution)/shard_map/ppermute | solution.py:27
  26.2 1.6 collective-permute-start.10
  27.8 1.5 collective-permute-start.11
  29.3 2.7 %collective-permute-done.4.refs_4_ = bf16[64,2176]{1,0:T(8,128)(2,1)S(1)} collective-permute-done((bf16[64,2176]{1,0:T(8,128)(2,1)S(1)}, bf16[64,2176]{1,0:T(8,128)(2,1)S(1)}, u32[]{:S(2)}, u32[]{:S(2)}) %collective-permute-start.4) | collective-permute-done | bytes 278560 | tf_op jit(solution)/shard_map/ppermute | solution.py:27
  32.1 1.6 collective-permute-start.8
  33.6 1.5 collective-permute-start.9
  35.2 2.5 %collective-permute-done.10.refs_7_ = bf16[64,2048]{1,0:T(8,128)(2,1)} collective-permute-done((bf16[64,2048]{1,0:T(8,128)(2,1)S(1)}, bf16[64,2048]{1,0:T(8,128)(2,1)}, u32[]{:S(2)}, u32[]{:S(2)}) %collective-permute-start.10) | collective-permute-done | bytes 262176 | tf_op jit(solution)/shard_map/ppermute | solution.py:27
  37.8 0.4 collective-permute-start.22
  38.2 4.5 %collective-permute-done.8.refs_6_ = bf16[64,2176]{1,0:T(8,128)(2,1)S(1)} collective-permute-done((bf16[64,2176]{1,0:T(8,128)(2,1)S(1)}, bf16[64,2176]{1,0:T(8,128)(2,1)S(1)}, u32[]{:S(2)}, u32[]{:S(2)}) %collective-permute-start.8) | collective-permute-done | bytes 278560 | tf_op jit(solution)/shard_map/ppermute | solution.py:27
  42.8 0.5 collective-permute-start.25
  43.4 0.4 collective-permute-start.27
  43.8 1.5 collective-permute-start.12
  45.3 0.9 collective-permute-start.13
  46.2 0.5 collective-permute-start.15
  47.0 0.4 copy-done.7
  47.4 8.9 %early.1 = (bf16[4,144,2048]{2,1,0:T(8,128)(2,1)}, bf16[1,1024,576]{2,1,0:T(8,128)(2,1)}, f32[4,144,1]{2,1,0:T(8,128)}) custom-call(s32[1]{0:T(128)} %bitcast.2.first_ref, bf16[64,2176]{1,0:T(8,128)(2,1)} %get-tuple-element.45.refs_0_, bf16[64,2048]{1,0:T(8,128)(2,1)} %get-tuple-element.47.refs_1_, bf16[64,2176]{1,0:T(8,128)(2,1)} %copy-done.1, ...), custom_call_target="tpu_custom_call" | custom-call | flops 1 | bytes 1 | tf_op jit(solution)/shard_map/early/pallas_call | solution.py:347
  56.4 1.8 %collective-permute-done.13.refs_7_ = bf16[64,2048]{1,0:T(8,128)(2,1)} collective-permute-done((bf16[64,2048]{1,0:T(8,128)(2,1)}, bf16[64,2048]{1,0:T(8,128)(2,1)}, u32[]{:S(2)}, u32[]{:S(2)}) %collective-permute-start.13) | collective-permute-done | bytes 262176 | tf_op jit(solution)/shard_map/ppermute | solution.py:32
  58.2 0.5 collective-permute-start.18
  58.8 0.4 collective-permute-start.19
  59.3 0.4 collective-permute-done.16.refs_10_
  59.7 1.4 collective-permute-done.19.refs_13_
  61.1 0.4 collective-permute-done.29.refs_15_
  61.9 0.3 copy-done.17
  62.3 48.4 %experts.1 = (bf16[128,2048]{1,0:T(8,128)(2,1)}, bf16[128,2048]{1,0:T(8,128)(2,1)}, bf16[128,2048]{1,0:T(8,128)(2,1)}, bf16[128,2048]{1,0:T(8,128)(2,1)}, bf16[1...) custom-call(s32[1]{0:T(128)} %bitcast.2.first_ref, ...), custom_call_target="tpu_custom_call" | custom-call | flops 19931332608 | bytes 77594624 | tf_op jit(solution)/shard_map/experts/pallas_call | solution.py:382
  110.9 0.4 collective-permute-start.33
  111.4 1.5 collective-permute-done.36
  113.0 1.2 add_convert_fusion.4
  114.2 1.6 collective-permute-start.38
  115.8 0.4 collective-permute-start.34
  116.4 1.2 add_convert_fusion.2
  117.5 0.6 collective-permute-start.43
  118.1 10.9 %collective-permute-done.38 = bf16[128,2048]{1,0:T(8,128)(2,1)S(1)} collective-permute-done((bf16[128,2048]{1,0:T(8,128)(2,1)S(1)}, bf16[128,2048]{1,0:T(8,128)(2,1)S(1)}, u32[]{:S(2)}, u32[]{:S(2)}) %collective-permute-start.38) | collective-permute-done | bytes 524320 | tf_op jit(solution)/shard_map/ppermute | solution.py:32
  129.0 1.3 add_convert_fusion.3
  130.3 1.8 collective-permute-start.39
  132.1 1.2 add_convert_fusion.6
  133.3 1.6 collective-permute-start.35
  134.8 1.2 add_convert_fusion.7
  136.1 4.1 %collective-permute-done.43 = bf16[128,2048]{1,0:T(8,128)(2,1)S(1)} collective-permute-done((bf16[128,2048]{1,0:T(8,128)(2,1)S(1)}, bf16[128,2048]{1,0:T(8,128)(2,1)S(1)}, u32[]{:S(2)}, u32[]{:S(2)}) %collective-permute-start.43) | collective-permute-done | bytes 524320 | tf_op jit(solution)/shard_map/ppermute | solution.py:32
  140.2 1.5 collective-permute-start.32
  141.7 1.4 collective-permute-done.39
  143.2 1.4 add_convert_fusion.1
  144.5 3.6 %collective-permute-start.44 = (bf16[128,2048]{1,0:T(8,128)(2,1)S(1)}, bf16[128,2048]{1,0:T(8,128)(2,1)}, u32[]{:S(2)}, u32[]{:S(2)}) collective-permute-start(bf16[128,2048]{1,0:T(8,128)(2,1)S(1)} %add_convert_fusion.1), channel_id=1, source_target_pairs={{0,3},{1,0},{2,1},{3,2},{4,7},{5,4},{6,5},{7,6},{8,11},{9,8},{10,9... | collective-permute-start | bytes 1572872 | tf_op jit(solution)/shard_map/ppermute | solution.py:27
  148.1 3.3 %collective-permute-done.35 = bf16[128,2048]{1,0:T(8,128)(2,1)S(1)} collective-permute-done((bf16[128,2048]{1,0:T(8,128)(2,1)S(1)}, bf16[128,2048]{1,0:T(8,128)(2,1)S(1)}, u32[]{:S(2)}, u32[]{:S(2)}) %collective-permute-start.35) | collective-permute-done | bytes 524320 | tf_op jit(solution)/shard_map/ppermute | solution.py:32
  151.5 2.1 %add_convert_fusion.5 = bf16[128,2048]{1,0:T(8,128)(2,1)} fusion(bf16[128,2048]{1,0:T(8,128)(2,1)S(1)} %collective-permute-done.35, bf16[128,2048]{1,0:T(8,128)(2,1)S(1)} %collective-permute-done.34, bf16[128,2048]{1,0:T(8,128)(2,1)} %get-tuple-element.69), kind=kLoop, calls=%fused_computation.11 | loop fusion | flops 1572864 | bytes 2097152 | tf_op jit(solution)/shard_map/convert_element_type | solution.py:50
  153.5 0.9 collective-permute-start.40
  154.5 6.0 %collective-permute-done.44 = bf16[128,2048]{1,0:T(8,128)(2,1)} collective-permute-done((bf16[128,2048]{1,0:T(8,128)(2,1)S(1)}, bf16[128,2048]{1,0:T(8,128)(2,1)}, u32[]{:S(2)}, u32[]{:S(2)}) %collective-permute-start.44) | collective-permute-done | bytes 524320 | tf_op jit(solution)/shard_map/ppermute | solution.py:27
  160.5 1.3 fusion.3
  161.8 0.3 collective-permute-done.32
  162.1 7.4 %collective-permute-done.40 = bf16[128,2048]{1,0:T(8,128)(2,1)S(1)} collective-permute-done((bf16[128,2048]{1,0:T(8,128)(2,1)}, bf16[128,2048]{1,0:T(8,128)(2,1)S(1)}, u32[]{:S(2)}, u32[]{:S(2)}) %collective-permute-start.40) | collective-permute-done | bytes 524320 | tf_op jit(solution)/shard_map/ppermute | solution.py:27
  169.5 1.8 %fusion.2 = bf16[32,2048]{1,0:T(8,128)(2,1)S(1)} fusion(f32[32,2048]{1,0:T(8,128)S(1)} %fusion.3, bf16[128,2048]{1,0:T(8,128)(2,1)S(1)} %collective-permute-done.40, bf16[128,2048]{1,0:T(8,128)(2,1)S(1)} %collective-permute-done.32, bf16[128,2048]{1,0:T(8,128)(2,1)S(1)} %collective-permute-done.31, bf16[128,2048]{1,0:T(8,128)(2,1)} %get-tuple-element.64, ...), kind=kOutput, calls=%fused_computation.4 | convolution fusion | flops 103157760 | bytes 3014784 | tf_op jit(solution)/shard_map/dot_general | solution.py:448
  171.4 3.4 %collective-permute-start.45 = (bf16[32,2048]{1,0:T(8,128)(2,1)S(1)}, bf16[32,2048]{1,0:T(8,128)(2,1)S(1)}, u32[]{:S(2)}, u32[]{:S(2)}) collective-permute-start(bf16[32,2048]{1,0:T(8,128)(2,1)S(1)} %fusion.2), channel_id=1, source_target_pairs={{0,16},{1,17},{2,18},{3,19},{4,20},{5,21},{6,22},{7,23},{8,24},{9,... | collective-permute-start | bytes 393224 | tf_op jit(solution)/shard_map/ppermute | solution.py:22
  174.9 2.4 %collective-permute-done.45 = bf16[32,2048]{1,0:T(8,128)(2,1)S(1)} collective-permute-done((bf16[32,2048]{1,0:T(8,128)(2,1)S(1)}, bf16[32,2048]{1,0:T(8,128)(2,1)S(1)}, u32[]{:S(2)}, u32[]{:S(2)}) %collective-permute-start.45) | collective-permute-done | bytes 131104 | tf_op jit(solution)/shard_map/ppermute | solution.py:22
  177.3 2.7 %fusion.1 = bf16[128,2048]{1,0:T(8,128)(2,1)} fusion(bf16[32,2048]{1,0:T(8,128)(2,1)S(1)} %collective-permute-done.45, bf16[128,2048]{1,0:T(8,128)(2,1)} %collective-permute-done.44, pred[128]{0:T(512)(128)(4,1)S(1)} %fusion.4, pred[]{:T(512)S(6)} %eq.30, bf16[128,2048]{1,0:T(8,128)(2,1)S(1)} %collective-permute-done.40, ...), kind=kOutput, calls=%fused_computation.2 | convolution fusion | flops 20713472 | bytes 3801345 | tf_op jit(solution)/shard_map/dot_general | solution.py:461
  (92 shorter events, 2.5 us)
Async XLA Ops:
  2.0 12.4 %collective-permute-start.2 = (bf16[64,2048]{1,0:T(8,128)(2,1)}, bf16[64,2048]{1,0:T(8,128)(2,1)S(1)}, u32[]{:S(2)}, u32[]{:S(2)}) collective-permute-start(bf16[64,2048]{1,0:T(8,128)(2,1)} %get-tuple-element.47.refs_1_), channel_id=1, source_target_pairs={{0,1},{1,2},{2,3},{3,0},{4,5},{5,6},{6,7},{7,4},{8,9},{9,10},{10,1... | collective-permute-start | bytes 786440 | tf_op jit(solution)/shard_map/ppermute | solution.py:27
  5.1 9.5 %collective-permute-start.3 = (bf16[64,2048]{1,0:T(8,128)(2,1)}, bf16[64,2048]{1,0:T(8,128)(2,1)}, u32[]{:S(2)}, u32[]{:S(2)}) collective-permute-start(bf16[64,2048]{1,0:T(8,128)(2,1)} %get-tuple-element.47.refs_1_), channel_id=1, source_target_pairs={{0,8},{4,12},{8,0},{12,4},{1,9},{5,13},{9,1},{13,5},{2,10},{6,14},... | collective-permute-start | bytes 786440 | tf_op jit(solution)/shard_map/ppermute | solution.py:32
  6.6 13.8 %collective-permute-start = (bf16[64,2176]{1,0:T(8,128)(2,1)}, bf16[64,2176]{1,0:T(8,128)(2,1)S(1)}, u32[]{:S(2)}, u32[]{:S(2)}) collective-permute-start(bf16[64,2176]{1,0:T(8,128)(2,1)} %get-tuple-element.45.refs_0_), channel_id=1, source_target_pairs={{0,1},{1,2},{2,3},{3,0},{4,5},{5,6},{6,7},{7,4},{8,9},{9,10},{10,1... | collective-permute-start | bytes 835592 | tf_op jit(solution)/shard_map/ppermute | solution.py:27
  8.2 12.3 %collective-permute-start.1 = (bf16[64,2176]{1,0:T(8,128)(2,1)}, bf16[64,2176]{1,0:T(8,128)(2,1)S(1)}, u32[]{:S(2)}, u32[]{:S(2)}) collective-permute-start(bf16[64,2176]{1,0:T(8,128)(2,1)} %get-tuple-element.45.refs_0_), channel_id=1, source_target_pairs={{0,8},{4,12},{8,0},{12,4},{1,9},{5,13},{9,1},{13,5},{2,10},{6,14},... | collective-permute-start | bytes 835592 | tf_op jit(solution)/shard_map/ppermute | solution.py:32
  14.4 32.3 %copy-start.18 = (bf16[64,2048]{1,0:T(8,128)(2,1)}, bf16[64,2048]{1,0:T(8,128)(2,1)S(1)}, u32[]{:S(2)}) copy-start(bf16[64,2048]{1,0:T(8,128)(2,1)S(1)} %collective-permute-done.2.refs_3_) | copy-start | bytes 786436
  14.6 11.4 %collective-permute-start.6 = (bf16[64,2048]{1,0:T(8,128)(2,1)S(1)}, bf16[64,2048]{1,0:T(8,128)(2,1)S(1)}, u32[]{:S(2)}, u32[]{:S(2)}) collective-permute-start(bf16[64,2048]{1,0:T(8,128)(2,1)S(1)} %collective-permute-done.2.refs_3_), channel_id=1, source_target_pairs={{0,1},{1,2},{2,3},{3,0},{4,5},{5,6},{6,7},{7,4},{8,9},{9,10},{10,1... | collective-permute-start | bytes 786440 | tf_op jit(solution)/shard_map/ppermute | solution.py:27
  16.2 10.0 %collective-permute-start.7 = (bf16[64,2048]{1,0:T(8,128)(2,1)S(1)}, bf16[64,2048]{1,0:T(8,128)(2,1)}, u32[]{:S(2)}, u32[]{:S(2)}) collective-permute-start(bf16[64,2048]{1,0:T(8,128)(2,1)S(1)} %collective-permute-done.2.refs_3_), channel_id=1, source_target_pairs={{0,8},{4,12},{8,0},{12,4},{1,9},{5,13},{9,1},{13,5},{2,10},{6,14},... | collective-permute-start | bytes 786440 | tf_op jit(solution)/shard_map/ppermute | solution.py:32
  20.4 26.6 %copy-start.1 = (bf16[64,2176]{1,0:T(8,128)(2,1)}, bf16[64,2176]{1,0:T(8,128)(2,1)S(1)}, u32[]{:S(2)}) copy-start(bf16[64,2176]{1,0:T(8,128)(2,1)S(1)} %collective-permute-done.refs_2_) | copy-start | bytes 835588
  20.5 41.0 %copy-start.8 = (bf16[64,2176]{1,0:T(8,128)(2,1)}, bf16[64,2176]{1,0:T(8,128)(2,1)S(1)}, u32[]{:S(2)}) copy-start(bf16[64,2176]{1,0:T(8,128)(2,1)S(1)} %collective-permute-done.1.refs_0_) | copy-start | bytes 835588
  20.5 11.5 %collective-permute-start.4 = (bf16[64,2176]{1,0:T(8,128)(2,1)S(1)}, bf16[64,2176]{1,0:T(8,128)(2,1)S(1)}, u32[]{:S(2)}, u32[]{:S(2)}) collective-permute-start(bf16[64,2176]{1,0:T(8,128)(2,1)S(1)} %collective-permute-done.refs_2_), channel_id=1, source_target_pairs={{0,1},{1,2},{2,3},{3,0},{4,5},{5,6},{6,7},{7,4},{8,9},{9,10},{10,1... | collective-permute-start | bytes 835592 | tf_op jit(solution)/shard_map/ppermute | solution.py:27
  22.1 10.0 %collective-permute-start.5 = (bf16[64,2176]{1,0:T(8,128)(2,1)S(1)}, bf16[64,2176]{1,0:T(8,128)(2,1)S(1)}, u32[]{:S(2)}, u32[]{:S(2)}) collective-permute-start(bf16[64,2176]{1,0:T(8,128)(2,1)S(1)} %collective-permute-done.refs_2_), channel_id=1, source_target_pairs={{0,8},{4,12},{8,0},{12,4},{1,9},{5,13},{9,1},{13,5},{2,10},{6,14},... | collective-permute-start | bytes 835592 | tf_op jit(solution)/shard_map/ppermute | solution.py:32
  23.6 11.6 %collective-permute-start.21 = (bf16[64,2048]{1,0:T(8,128)(2,1)}, bf16[64,2048]{1,0:T(8,128)(2,1)}, u32[]{:S(2)}, u32[]{:S(2)}) collective-permute-start(bf16[64,2048]{1,0:T(8,128)(2,1)} %get-tuple-element.47.refs_1_), channel_id=1, source_target_pairs={{0,4},{4,0},{8,12},{12,8},{1,5},{5,1},{9,13},{13,9},{2,6},{6,2},{1... | collective-permute-start | bytes 786440 | tf_op jit(solution)/shard_map/ppermute | solution.py:32
  26.0 20.9 %copy-start.19 = (bf16[64,2048]{1,0:T(8,128)(2,1)}, bf16[64,2048]{1,0:T(8,128)(2,1)S(1)}, u32[]{:S(2)}) copy-start(bf16[64,2048]{1,0:T(8,128)(2,1)S(1)} %collective-permute-done.6.refs_5_) | copy-start | bytes 786436
  26.2 11.5 %collective-permute-start.10 = (bf16[64,2048]{1,0:T(8,128)(2,1)S(1)}, bf16[64,2048]{1,0:T(8,128)(2,1)}, u32[]{:S(2)}, u32[]{:S(2)}) collective-permute-start(bf16[64,2048]{1,0:T(8,128)(2,1)S(1)} %collective-permute-done.6.refs_5_), channel_id=1, source_target_pairs={{0,1},{1,2},{2,3},{3,0},{4,5},{5,6},{6,7},{7,4},{8,9},{9,10},{10,1... | collective-permute-start | bytes 786440 | tf_op jit(solution)/shard_map/ppermute | solution.py:27
  27.8 10.0 %collective-permute-start.11 = (bf16[64,2048]{1,0:T(8,128)(2,1)S(1)}, bf16[64,2048]{1,0:T(8,128)(2,1)}, u32[]{:S(2)}, u32[]{:S(2)}) collective-permute-start(bf16[64,2048]{1,0:T(8,128)(2,1)S(1)} %collective-permute-done.6.refs_5_), channel_id=1, source_target_pairs={{0,8},{4,12},{8,0},{12,4},{1,9},{5,13},{9,1},{13,5},{2,10},{6,14},... | collective-permute-start | bytes 786440 | tf_op jit(solution)/shard_map/ppermute | solution.py:32
  32.0 15.0 %copy-start.2 = (bf16[64,2176]{1,0:T(8,128)(2,1)}, bf16[64,2176]{1,0:T(8,128)(2,1)S(1)}, u32[]{:S(2)}) copy-start(bf16[64,2176]{1,0:T(8,128)(2,1)S(1)} %collective-permute-done.4.refs_4_) | copy-start | bytes 835588
  32.1 29.4 %copy-start.9 = (bf16[64,2176]{1,0:T(8,128)(2,1)}, bf16[64,2176]{1,0:T(8,128)(2,1)S(1)}, u32[]{:S(2)}) copy-start(bf16[64,2176]{1,0:T(8,128)(2,1)S(1)} %collective-permute-done.5.refs_2_) | copy-start | bytes 835588
  32.1 10.7 %collective-permute-start.8 = (bf16[64,2176]{1,0:T(8,128)(2,1)S(1)}, bf16[64,2176]{1,0:T(8,128)(2,1)S(1)}, u32[]{:S(2)}, u32[]{:S(2)}) collective-permute-start(bf16[64,2176]{1,0:T(8,128)(2,1)S(1)} %collective-permute-done.4.refs_4_), channel_id=1, source_target_pairs={{0,1},{1,2},{2,3},{3,0},{4,5},{5,6},{6,7},{7,4},{8,9},{9,10},{10,1... | collective-permute-start | bytes 835592 | tf_op jit(solution)/shard_map/ppermute | solution.py:27
  33.6 9.1 %collective-permute-start.9 = (bf16[64,2176]{1,0:T(8,128)(2,1)S(1)}, bf16[64,2176]{1,0:T(8,128)(2,1)S(1)}, u32[]{:S(2)}, u32[]{:S(2)}) collective-permute-start(bf16[64,2176]{1,0:T(8,128)(2,1)S(1)} %collective-permute-done.4.refs_4_), channel_id=1, source_target_pairs={{0,8},{4,12},{8,0},{12,4},{1,9},{5,13},{9,1},{13,5},{2,10},{6,14},... | collective-permute-start | bytes 835592 | tf_op jit(solution)/shard_map/ppermute | solution.py:32
  35.2 8.1 %collective-permute-start.20 = (bf16[64,2176]{1,0:T(8,128)(2,1)}, bf16[64,2176]{1,0:T(8,128)(2,1)S(1)}, u32[]{:S(2)}, u32[]{:S(2)}) collective-permute-start(bf16[64,2176]{1,0:T(8,128)(2,1)} %get-tuple-element.45.refs_0_), channel_id=1, source_target_pairs={{0,4},{4,0},{8,12},{12,8},{1,5},{5,1},{9,13},{13,9},{2,6},{6,2},{1... | collective-permute-start | bytes 835592 | tf_op jit(solution)/shard_map/ppermute | solution.py:32
  37.7 5.6 %collective-permute-start.23 = (bf16[64,2048]{1,0:T(8,128)(2,1)S(1)}, bf16[64,2048]{1,0:T(8,128)(2,1)S(1)}, u32[]{:S(2)}, u32[]{:S(2)}) collective-permute-start(bf16[64,2048]{1,0:T(8,128)(2,1)S(1)} %collective-permute-done.2.refs_3_), channel_id=1, source_target_pairs={{0,4},{4,0},{8,12},{12,8},{1,5},{5,1},{9,13},{13,9},{2,6},{6,2},{1... | collective-permute-start | bytes 786440 | tf_op jit(solution)/shard_map/ppermute | solution.py:32
  37.8 6.0 %collective-permute-start.22 = (bf16[64,2176]{1,0:T(8,128)(2,1)S(1)}, bf16[64,2176]{1,0:T(8,128)(2,1)S(1)}, u32[]{:S(2)}, u32[]{:S(2)}) collective-permute-start(bf16[64,2176]{1,0:T(8,128)(2,1)S(1)} %collective-permute-done.refs_2_), channel_id=1, source_target_pairs={{0,4},{4,0},{8,12},{12,8},{1,5},{5,1},{9,13},{13,9},{2,6},{6,2},{1... | collective-permute-start | bytes 835592 | tf_op jit(solution)/shard_map/ppermute | solution.py:32
  42.7 4.2 %copy-start.3 = (bf16[64,2176]{1,0:T(8,128)(2,1)}, bf16[64,2176]{1,0:T(8,128)(2,1)S(1)}, u32[]{:S(2)}) copy-start(bf16[64,2176]{1,0:T(8,128)(2,1)S(1)} %collective-permute-done.8.refs_6_) | copy-start | bytes 835588
  42.7 3.5 %collective-permute-start.24 = (bf16[64,2176]{1,0:T(8,128)(2,1)S(1)}, bf16[64,2176]{1,0:T(8,128)(2,1)S(1)}, u32[]{:S(2)}, u32[]{:S(2)}) collective-permute-start(bf16[64,2176]{1,0:T(8,128)(2,1)S(1)} %collective-permute-done.4.refs_4_), channel_id=1, source_target_pairs={{0,4},{4,0},{8,12},{12,8},{1,5},{5,1},{9,13},{13,9},{2,6},{6,2},{1... | collective-permute-start | bytes 835592 | tf_op jit(solution)/shard_map/ppermute | solution.py:32
  42.8 18.7 %copy-start.10 = (bf16[64,2176]{1,0:T(8,128)(2,1)}, bf16[64,2176]{1,0:T(8,128)(2,1)S(1)}, u32[]{:S(2)}) copy-start(bf16[64,2176]{1,0:T(8,128)(2,1)S(1)} %collective-permute-done.9.refs_4_) | copy-start | bytes 835588
  42.8 2.5 %collective-permute-start.25 = (bf16[64,2048]{1,0:T(8,128)(2,1)S(1)}, bf16[64,2048]{1,0:T(8,128)(2,1)S(1)}, u32[]{:S(2)}, u32[]{:S(2)}) collective-permute-start(bf16[64,2048]{1,0:T(8,128)(2,1)S(1)} %collective-permute-done.6.refs_5_), channel_id=1, source_target_pairs={{0,4},{4,0},{8,12},{12,8},{1,5},{5,1},{9,13},{13,9},{2,6},{6,2},{1... | collective-permute-start | bytes 786440 | tf_op jit(solution)/shard_map/ppermute | solution.py:32
  43.3 3.7 %copy-start.4 = (bf16[64,2176]{1,0:T(8,128)(2,1)}, bf16[64,2176]{1,0:T(8,128)(2,1)S(1)}, u32[]{:S(2)}) copy-start(bf16[64,2176]{1,0:T(8,128)(2,1)S(1)} %collective-permute-done.20.refs_8_) | copy-start | bytes 835588
  43.3 3.5 %collective-permute-start.26 = (bf16[64,2176]{1,0:T(8,128)(2,1)S(1)}, bf16[64,2176]{1,0:T(8,128)(2,1)S(1)}, u32[]{:S(2)}, u32[]{:S(2)}) collective-permute-start(bf16[64,2176]{1,0:T(8,128)(2,1)S(1)} %collective-permute-done.8.refs_6_), channel_id=1, source_target_pairs={{0,4},{4,0},{8,12},{12,8},{1,5},{5,1},{9,13},{13,9},{2,6},{6,2},{1... | collective-permute-start | bytes 835592 | tf_op jit(solution)/shard_map/ppermute | solution.py:32
  43.4 3.5 %copy-start.20 = (bf16[64,2048]{1,0:T(8,128)(2,1)}, bf16[64,2048]{1,0:T(8,128)(2,1)S(1)}, u32[]{:S(2)}) copy-start(bf16[64,2048]{1,0:T(8,128)(2,1)S(1)} %collective-permute-done.23.refs_11_) | copy-start | bytes 786436
  43.4 2.9 %collective-permute-start.27 = (bf16[64,2048]{1,0:T(8,128)(2,1)}, bf16[64,2048]{1,0:T(8,128)(2,1)S(1)}, u32[]{:S(2)}, u32[]{:S(2)}) collective-permute-start(bf16[64,2048]{1,0:T(8,128)(2,1)} %collective-permute-done.10.refs_7_), channel_id=1, source_target_pairs={{0,4},{4,0},{8,12},{12,8},{1,5},{5,1},{9,13},{13,9},{2,6},{6,2},{1... | collective-permute-start | bytes 786440 | tf_op jit(solution)/shard_map/ppermute | solution.py:32
  43.8 3.2 %copy-start.5 = (bf16[64,2176]{1,0:T(8,128)(2,1)}, bf16[64,2176]{1,0:T(8,128)(2,1)S(1)}, u32[]{:S(2)}) copy-start(bf16[64,2176]{1,0:T(8,128)(2,1)S(1)} %collective-permute-done.22.refs_10_) | copy-start | bytes 835588
  43.8 14.4 %collective-permute-start.12 = (bf16[64,2176]{1,0:T(8,128)(2,1)S(1)}, bf16[64,2176]{1,0:T(8,128)(2,1)S(1)}, u32[]{:S(2)}, u32[]{:S(2)}) collective-permute-start(bf16[64,2176]{1,0:T(8,128)(2,1)S(1)} %collective-permute-done.8.refs_6_), channel_id=1, source_target_pairs={{0,8},{4,12},{8,0},{12,4},{1,9},{5,13},{9,1},{13,5},{2,10},{6,14},... | collective-permute-start | bytes 835592 | tf_op jit(solution)/shard_map/ppermute | solution.py:32
  45.3 1.6 copy-start.21
  45.3 12.8 %collective-permute-start.13 = (bf16[64,2048]{1,0:T(8,128)(2,1)}, bf16[64,2048]{1,0:T(8,128)(2,1)}, u32[]{:S(2)}, u32[]{:S(2)}) collective-permute-start(bf16[64,2048]{1,0:T(8,128)(2,1)} %collective-permute-done.10.refs_7_), channel_id=1, source_target_pairs={{0,8},{4,12},{8,0},{12,4},{1,9},{5,13},{9,1},{13,5},{2,10},{6,14},... | collective-permute-start | bytes 786440 | tf_op jit(solution)/shard_map/ppermute | solution.py:32
  46.2 12.6 %collective-permute-start.14 = (bf16[64,2176]{1,0:T(8,128)(2,1)S(1)}, bf16[64,2176]{1,0:T(8,128)(2,1)S(1)}, u32[]{:S(2)}, u32[]{:S(2)}) collective-permute-start(bf16[64,2176]{1,0:T(8,128)(2,1)S(1)} %collective-permute-done.1.refs_0_), channel_id=1, source_target_pairs={{0,4},{4,0},{8,12},{12,8},{1,5},{5,1},{9,13},{13,9},{2,6},{6,2},{1... | collective-permute-start | bytes 835592 | tf_op jit(solution)/shard_map/ppermute | solution.py:32
  46.2 12.4 %collective-permute-start.15 = (bf16[64,2048]{1,0:T(8,128)(2,1)}, bf16[64,2048]{1,0:T(8,128)(2,1)}, u32[]{:S(2)}, u32[]{:S(2)}) collective-permute-start(bf16[64,2048]{1,0:T(8,128)(2,1)} %collective-permute-done.3.refs_1_), channel_id=1, source_target_pairs={{0,4},{4,0},{8,12},{12,8},{1,5},{5,1},{9,13},{13,9},{2,6},{6,2},{1... | collective-permute-start | bytes 786440 | tf_op jit(solution)/shard_map/ppermute | solution.py:32
  46.7 12.5 %collective-permute-start.17 = (bf16[64,2048]{1,0:T(8,128)(2,1)}, bf16[64,2048]{1,0:T(8,128)(2,1)}, u32[]{:S(2)}, u32[]{:S(2)}) collective-permute-start(bf16[64,2048]{1,0:T(8,128)(2,1)} %collective-permute-done.7.refs_3_), channel_id=1, source_target_pairs={{0,4},{4,0},{8,12},{12,8},{1,5},{5,1},{9,13},{13,9},{2,6},{6,2},{1... | collective-permute-start | bytes 786440 | tf_op jit(solution)/shard_map/ppermute | solution.py:32
  58.2 1.6 collective-permute-start.16
  58.2 3.3 %copy-start.11 = (bf16[64,2176]{1,0:T(8,128)(2,1)}, bf16[64,2176]{1,0:T(8,128)(2,1)S(1)}, u32[]{:S(2)}) copy-start(bf16[64,2176]{1,0:T(8,128)(2,1)S(1)} %collective-permute-done.12.refs_6_) | copy-start | bytes 835588
  58.2 2.9 %collective-permute-start.18 = (bf16[64,2176]{1,0:T(8,128)(2,1)S(1)}, bf16[64,2176]{1,0:T(8,128)(2,1)S(1)}, u32[]{:S(2)}, u32[]{:S(2)}) collective-permute-start(bf16[64,2176]{1,0:T(8,128)(2,1)S(1)} %collective-permute-done.9.refs_4_), channel_id=1, source_target_pairs={{0,4},{4,0},{8,12},{12,8},{1,5},{5,1},{9,13},{13,9},{2,6},{6,2},{1... | collective-permute-start | bytes 835592 | tf_op jit(solution)/shard_map/ppermute | solution.py:32
  58.7 2.8 %collective-permute-start.28 = (bf16[64,2176]{1,0:T(8,128)(2,1)S(1)}, bf16[64,2176]{1,0:T(8,128)(2,1)S(1)}, u32[]{:S(2)}, u32[]{:S(2)}) collective-permute-start(bf16[64,2176]{1,0:T(8,128)(2,1)S(1)} %collective-permute-done.12.refs_6_), channel_id=1, source_target_pairs={{0,4},{4,0},{8,12},{12,8},{1,5},{5,1},{9,13},{13,9},{2,6},{6,2},{1... | collective-permute-start | bytes 835592 | tf_op jit(solution)/shard_map/ppermute | solution.py:32
  58.8 2.8 %copy-start.12 = (bf16[64,2176]{1,0:T(8,128)(2,1)}, bf16[64,2176]{1,0:T(8,128)(2,1)S(1)}, u32[]{:S(2)}) copy-start(bf16[64,2176]{1,0:T(8,128)(2,1)S(1)} %collective-permute-done.14.refs_8_) | copy-start | bytes 835588
  58.8 2.3 %collective-permute-start.19 = (bf16[64,2048]{1,0:T(8,128)(2,1)}, bf16[64,2048]{1,0:T(8,128)(2,1)S(1)}, u32[]{:S(2)}, u32[]{:S(2)}) collective-permute-start(bf16[64,2048]{1,0:T(8,128)(2,1)} %collective-permute-done.11.refs_5_), channel_id=1, source_target_pairs={{0,4},{4,0},{8,12},{12,8},{1,5},{5,1},{9,13},{13,9},{2,6},{6,2},{1... | collective-permute-start | bytes 786440 | tf_op jit(solution)/shard_map/ppermute | solution.py:32
  59.2 2.3 %collective-permute-start.29 = (bf16[64,2048]{1,0:T(8,128)(2,1)}, bf16[64,2048]{1,0:T(8,128)(2,1)S(1)}, u32[]{:S(2)}, u32[]{:S(2)}) collective-permute-start(bf16[64,2048]{1,0:T(8,128)(2,1)} %collective-permute-done.13.refs_7_), channel_id=1, source_target_pairs={{0,4},{4,0},{8,12},{12,8},{1,5},{5,1},{9,13},{13,9},{2,6},{6,2},{1... | collective-permute-start | bytes 786440 | tf_op jit(solution)/shard_map/ppermute | solution.py:32
  59.7 1.8 %copy-start.13 = (bf16[64,2176]{1,0:T(8,128)(2,1)}, bf16[64,2176]{1,0:T(8,128)(2,1)S(1)}, u32[]{:S(2)}) copy-start(bf16[64,2176]{1,0:T(8,128)(2,1)S(1)} %collective-permute-done.16.refs_10_) | copy-start | bytes 835588
  61.5 0.8 copy-start.15
  62.3 92.2 %copy-start.23 = (s32[1,2,32]{2,1,0:T(2,128)S(1)}, s32[1,2,32]{2,1,0:T(2,128)}, u32[]{:S(2)}) copy-start(s32[1,2,32]{2,1,0:T(2,128)} %param.12) | copy-start | bytes 772
  62.3 107.2 %copy-start = (bf16[128,2048]{1,0:T(8,128)(2,1)S(1)}, bf16[128,2048]{1,0:T(8,128)(2,1)}, u32[]{:S(2)}) copy-start(bf16[128,2048]{1,0:T(8,128)(2,1)} %tokens_ref.1) | copy-start | bytes 1572868
  110.7 2.2 %collective-permute-start.36 = (bf16[128,2048]{1,0:T(8,128)(2,1)}, bf16[128,2048]{1,0:T(8,128)(2,1)S(1)}, u32[]{:S(2)}, u32[]{:S(2)}) collective-permute-start(bf16[128,2048]{1,0:T(8,128)(2,1)} %get-tuple-element.76), channel_id=1, source_target_pairs={{0,4},{4,0},{8,12},{12,8},{1,5},{5,1},{9,13},{13,9},{2,6},{6,2},{1... | collective-permute-start | bytes 1572872 | tf_op jit(solution)/shard_map/ppermute | solution.py:32
  110.9 5.0 %collective-permute-start.33 = (bf16[128,2048]{1,0:T(8,128)(2,1)}, bf16[128,2048]{1,0:T(8,128)(2,1)S(1)}, u32[]{:S(2)}, u32[]{:S(2)}) collective-permute-start(bf16[128,2048]{1,0:T(8,128)(2,1)} %get-tuple-element.71), channel_id=1, source_target_pairs={{0,4},{4,0},{8,12},{12,8},{1,5},{5,1},{9,13},{13,9},{2,6},{6,2},{1... | collective-permute-start | bytes 1572872 | tf_op jit(solution)/shard_map/ppermute | solution.py:32
  111.2 5.0 %collective-permute-start.41 = (bf16[128,2048]{1,0:T(8,128)(2,1)}, bf16[128,2048]{1,0:T(8,128)(2,1)S(1)}, u32[]{:S(2)}, u32[]{:S(2)}) collective-permute-start(bf16[128,2048]{1,0:T(8,128)(2,1)} %get-tuple-element.82), channel_id=1, source_target_pairs={{0,4},{4,0},{8,12},{12,8},{1,5},{5,1},{9,13},{13,9},{2,6},{6,2},{1... | collective-permute-start | bytes 1572872 | tf_op jit(solution)/shard_map/ppermute | solution.py:32
  112.9 4.7 %collective-permute-start.37 = (bf16[128,2048]{1,0:T(8,128)(2,1)}, bf16[128,2048]{1,0:T(8,128)(2,1)S(1)}, u32[]{:S(2)}, u32[]{:S(2)}) collective-permute-start(bf16[128,2048]{1,0:T(8,128)(2,1)} %get-tuple-element.77), channel_id=1, source_target_pairs={{0,4},{4,0},{8,12},{12,8},{1,5},{5,1},{9,13},{13,9},{2,6},{6,2},{1... | collective-permute-start | bytes 1572872 | tf_op jit(solution)/shard_map/ppermute | solution.py:32
  114.2 14.8 %collective-permute-start.38 = (bf16[128,2048]{1,0:T(8,128)(2,1)S(1)}, bf16[128,2048]{1,0:T(8,128)(2,1)S(1)}, u32[]{:S(2)}, u32[]{:S(2)}) collective-permute-start(bf16[128,2048]{1,0:T(8,128)(2,1)S(1)} %add_convert_fusion.4), channel_id=1, source_target_pairs={{0,8},{4,12},{8,0},{12,4},{1,9},{5,13},{9,1},{13,5},{2,10},{6,14},... | collective-permute-start | bytes 1572872 | tf_op jit(solution)/shard_map/ppermute | solution.py:32
  115.8 17.5 %collective-permute-start.30 = (bf16[128,2048]{1,0:T(8,128)(2,1)}, bf16[128,2048]{1,0:T(8,128)(2,1)S(1)}, u32[]{:S(2)}, u32[]{:S(2)}) collective-permute-start(bf16[128,2048]{1,0:T(8,128)(2,1)} %get-tuple-element.66), channel_id=1, source_target_pairs={{0,4},{4,0},{8,12},{12,8},{1,5},{5,1},{9,13},{13,9},{2,6},{6,2},{1... | collective-permute-start | bytes 1572872 | tf_op jit(solution)/shard_map/ppermute | solution.py:32
  115.8 32.3 %collective-permute-start.34 = (bf16[128,2048]{1,0:T(8,128)(2,1)}, bf16[128,2048]{1,0:T(8,128)(2,1)S(1)}, u32[]{:S(2)}, u32[]{:S(2)}) collective-permute-start(bf16[128,2048]{1,0:T(8,128)(2,1)} %get-tuple-element.72), channel_id=1, source_target_pairs={{0,4},{4,0},{8,12},{12,8},{1,5},{5,1},{9,13},{13,9},{2,6},{6,2},{1... | collective-permute-start | bytes 1572872 | tf_op jit(solution)/shard_map/ppermute | solution.py:32
  116.3 19.7 %collective-permute-start.42 = (bf16[128,2048]{1,0:T(8,128)(2,1)}, bf16[128,2048]{1,0:T(8,128)(2,1)S(1)}, u32[]{:S(2)}, u32[]{:S(2)}) collective-permute-start(bf16[128,2048]{1,0:T(8,128)(2,1)} %get-tuple-element.83), channel_id=1, source_target_pairs={{0,4},{4,0},{8,12},{12,8},{1,5},{5,1},{9,13},{13,9},{2,6},{6,2},{1... | collective-permute-start | bytes 1572872 | tf_op jit(solution)/shard_map/ppermute | solution.py:32
  117.5 22.7 %collective-permute-start.43 = (bf16[128,2048]{1,0:T(8,128)(2,1)S(1)}, bf16[128,2048]{1,0:T(8,128)(2,1)S(1)}, u32[]{:S(2)}, u32[]{:S(2)}) collective-permute-start(bf16[128,2048]{1,0:T(8,128)(2,1)S(1)} %add_convert_fusion.2), channel_id=1, source_target_pairs={{0,8},{4,12},{8,0},{12,4},{1,9},{5,13},{9,1},{13,5},{2,10},{6,14},... | collective-permute-start | bytes 1572872 | tf_op jit(solution)/shard_map/ppermute | solution.py:32
  130.3 12.9 %collective-permute-start.39 = (bf16[128,2048]{1,0:T(8,128)(2,1)S(1)}, bf16[128,2048]{1,0:T(8,128)(2,1)S(1)}, u32[]{:S(2)}, u32[]{:S(2)}) collective-permute-start(bf16[128,2048]{1,0:T(8,128)(2,1)S(1)} %add_convert_fusion.3), channel_id=1, source_target_pairs={{0,3},{1,0},{2,1},{3,2},{4,7},{5,4},{6,5},{7,6},{8,11},{9,8},{10,9... | collective-permute-start | bytes 1572872 | tf_op jit(solution)/shard_map/ppermute | solution.py:27
  133.3 18.2 %collective-permute-start.35 = (bf16[128,2048]{1,0:T(8,128)(2,1)S(1)}, bf16[128,2048]{1,0:T(8,128)(2,1)S(1)}, u32[]{:S(2)}, u32[]{:S(2)}) collective-permute-start(bf16[128,2048]{1,0:T(8,128)(2,1)S(1)} %add_convert_fusion.6), channel_id=1, source_target_pairs={{0,8},{4,12},{8,0},{12,4},{1,9},{5,13},{9,1},{13,5},{2,10},{6,14},... | collective-permute-start | bytes 1572872 | tf_op jit(solution)/shard_map/ppermute | solution.py:32
  136.0 25.8 %collective-permute-start.31 = (bf16[128,2048]{1,0:T(8,128)(2,1)}, bf16[128,2048]{1,0:T(8,128)(2,1)S(1)}, u32[]{:S(2)}, u32[]{:S(2)}) collective-permute-start(bf16[128,2048]{1,0:T(8,128)(2,1)} %get-tuple-element.67), channel_id=1, source_target_pairs={{0,4},{4,0},{8,12},{12,8},{1,5},{5,1},{9,13},{13,9},{2,6},{6,2},{1... | collective-permute-start | bytes 1572872 | tf_op jit(solution)/shard_map/ppermute | solution.py:32
  140.2 21.9 %collective-permute-start.32 = (bf16[128,2048]{1,0:T(8,128)(2,1)S(1)}, bf16[128,2048]{1,0:T(8,128)(2,1)S(1)}, u32[]{:S(2)}, u32[]{:S(2)}) collective-permute-start(bf16[128,2048]{1,0:T(8,128)(2,1)S(1)} %add_convert_fusion.7), channel_id=1, source_target_pairs={{0,8},{4,12},{8,0},{12,4},{1,9},{5,13},{9,1},{13,5},{2,10},{6,14},... | collective-permute-start | bytes 1572872 | tf_op jit(solution)/shard_map/ppermute | solution.py:32
  144.5 16.0 %collective-permute-start.44 = (bf16[128,2048]{1,0:T(8,128)(2,1)S(1)}, bf16[128,2048]{1,0:T(8,128)(2,1)}, u32[]{:S(2)}, u32[]{:S(2)}) collective-permute-start(bf16[128,2048]{1,0:T(8,128)(2,1)S(1)} %add_convert_fusion.1), channel_id=1, source_target_pairs={{0,3},{1,0},{2,1},{3,2},{4,7},{5,4},{6,5},{7,6},{8,11},{9,8},{10,9... | collective-permute-start | bytes 1572872 | tf_op jit(solution)/shard_map/ppermute | solution.py:27
  153.5 16.0 %collective-permute-start.40 = (bf16[128,2048]{1,0:T(8,128)(2,1)}, bf16[128,2048]{1,0:T(8,128)(2,1)S(1)}, u32[]{:S(2)}, u32[]{:S(2)}) collective-permute-start(bf16[128,2048]{1,0:T(8,128)(2,1)} %add_convert_fusion.5), channel_id=1, source_target_pairs={{0,1},{1,2},{2,3},{3,0},{4,5},{5,6},{6,7},{7,4},{8,9},{9,10},{10,1... | collective-permute-start | bytes 1572872 | tf_op jit(solution)/shard_map/ppermute | solution.py:27
  171.4 5.9 %collective-permute-start.45 = (bf16[32,2048]{1,0:T(8,128)(2,1)S(1)}, bf16[32,2048]{1,0:T(8,128)(2,1)S(1)}, u32[]{:S(2)}, u32[]{:S(2)}) collective-permute-start(bf16[32,2048]{1,0:T(8,128)(2,1)S(1)} %fusion.2), channel_id=1, source_target_pairs={{0,16},{1,17},{2,18},{3,19},{4,20},{5,21},{6,22},{7,23},{8,24},{9,... | collective-permute-start | bytes 393224 | tf_op jit(solution)/shard_map/ppermute | solution.py:22
  (6 other events, 4.5 us)
